TPU v7x, 256 devices: a whole 4x4x8 slice. The times are simulated.
256 devices in a mesh: mem: 8 (over x_lo, y), tile: 32 (over x_hi, z, core).
Axes of the slice: x: 4 (x_hi: 2, x_lo: 2; x = x_hi * 2 + x_lo), y: 4, z: 8, core: 2. Of those that a mesh axis runs over, the one named last changes fastest.
Arguments:
- members: float32 [80, 2, 524288], P('mem', None, 'tile'), may hold values from -6 to 6
- increment: float32 [2, 2097152], P(None, 'tile'), may hold values from -6 to 6
- fine_angles: float32 [2, 2097152], P(None, 'tile'), may hold values from -1.5 to 1.5
- coarse_angles: float32 [2, 524288], P(None, 'tile'), may hold values from -1.5 to 1.5
- remap_weights: bfloat16 [32, 128, 4, 256, 128], P('tile', 'mem'), may hold values from -0.1875 to 0.1875
- sources: int32 [32, 128, 4], P('tile', 'mem'), may hold values from 0 to 8191, as said below
- counts: int32 [32, 128], P('tile', 'mem'), may hold values from 2 to 4, as said below
Outputs:
- recentered: float32 [80, 2, 524288], P('mem', None, 'tile')
Inputs may be any that keep to these rules, and one draw needn't show every extreme that they name: `sources`: for entry [s, l], with g = 128 s + l, slots 0 and 1 name fine blocks 2 g and 2 g + 1; each further even slot names block (2 g - r) mod 8192 and each further odd slot block (2 g + 1 + r + 4096) mod 8192, each with its own r from 1 to 256. `counts`: every column shard holds a coarse block that uses all 4 slots.
All inputs are finite; a program needn't handle non-finite values.
Results may differ from a plain program's by a relative error of at most 0.0017.
Values may be sent and summed in bfloat16 or wider, within the bound.
No kernel may reach another device: no remote copies, remote signals or barrier semaphores. Data moves between devices by JAX's collectives and lax.ppermute only.
A program may use at most 64 MiB of HBM per device.

v0:
```python
import jax
import jax.numpy as jnp
from jax import lax
from jax.sharding import PartitionSpec as P


def to_vector(east_part, north_part, longitude, latitude):
    sin_lon, cos_lon = (jnp.sin(longitude), jnp.cos(longitude))
    sin_lat, cos_lat = (jnp.sin(latitude), jnp.cos(latitude))
    first = -sin_lon * east_part - sin_lat * cos_lon * north_part
    second = cos_lon * east_part - sin_lat * sin_lon * north_part
    third = cos_lat * north_part
    return (first, second, third)


def to_wind(first, second, third, longitude, latitude):
    sin_lon, cos_lon = (jnp.sin(longitude), jnp.cos(longitude))
    sin_lat, cos_lat = (jnp.sin(latitude), jnp.cos(latitude))
    east_part = -sin_lon * first + cos_lon * second
    north_part = -sin_lat * cos_lon * first - sin_lat * sin_lon * second + cos_lat * third
    return jnp.stack([east_part, north_part])


def shards(members, increment, fine_angles, coarse_angles, remap_weights, sources, counts):
    weights = remap_weights[0]
    source_ids = sources[0]
    slot_counts = counts[0]
    block_count = source_ids.shape[0]
    slot_total = source_ids.shape[1]
    fine_width = weights.shape[2]
    coarse_width = weights.shape[3]
    fine_blocks = increment.shape[1] // fine_width
    tile_index = lax.axis_index("tile")
    mem_index = lax.axis_index("mem")
    first, second, third = to_vector(
        increment[0].reshape(fine_blocks, fine_width),
        increment[1].reshape(fine_blocks, fine_width),
        fine_angles[0].reshape(fine_blocks, fine_width),
        fine_angles[1].reshape(fine_blocks, fine_width),
    )
    flat_blocks = (
        jnp.stack([first, second, third], axis=1)
        .astype(jnp.bfloat16)
        .reshape(fine_blocks, 3 * fine_width)
    )
    row_width = flat_blocks.shape[1]
    far_ids = source_ids[:, 2:].reshape(-1)
    far_count = far_ids.shape[0]
    start_rows = jnp.zeros((far_count, row_width), jnp.bfloat16)
    shard_piece = lax.all_gather(flat_blocks, "tile", axis=0, tiled=True)
    piece_rows = shard_piece.shape[0]
    inside = (far_ids >= 0) & (far_ids < piece_rows)
    taken = jnp.take(shard_piece, jnp.clip(far_ids, 0, piece_rows - 1), axis=0)
    fetched = jnp.where(inside[:, None], taken, start_rows)
    near_ids = source_ids[:, :2].reshape(-1) - tile_index * fine_blocks
    near_rows = jnp.take(flat_blocks, near_ids, axis=0)
    picked = jnp.concatenate(
        [near_rows.reshape(block_count, 2, -1), fetched.reshape(block_count, slot_total - 2, -1)],
        axis=1,
    )
    picked = picked.reshape(block_count, slot_total, 3, fine_width)
    live_slots = jnp.arange(slot_total, dtype=jnp.int32)[None, :] < slot_counts[:, None]
    picked = jnp.where(live_slots[:, :, None, None], picked, 0)
    coarse_cart = jnp.einsum("ikcf,ikfb->cib", picked, weights, preferred_element_type=jnp.float32)
    coarse_cart = coarse_cart.reshape(3, block_count * coarse_width)
    own_columns = block_count * coarse_width
    own_angles = lax.dynamic_slice_in_dim(coarse_angles, mem_index * own_columns, own_columns, 1)
    own_wind = to_wind(coarse_cart[0], coarse_cart[1], coarse_cart[2], own_angles[0], own_angles[1])
    member_count = members.shape[0] * lax.axis_size("mem")
    coarse_wind = lax.all_gather(own_wind, "mem", axis=1, tiled=True)
    member_total = lax.psum(jnp.sum(members, axis=0), "mem")
    member_mean = member_total / member_count
    return members - member_mean[None] + coarse_wind[None]


def solution(mesh):
    in_specs = (
        P("mem", None, "tile"),
        P(None, "tile"),
        P(None, "tile"),
        P(None, "tile"),
        P("tile", "mem", None, None, None),
        P("tile", "mem", None),
        P("tile", "mem"),
    )
    out_specs = P("mem", None, "tile")
    return jax.shard_map(shards, mesh=mesh, in_specs=in_specs, out_specs=out_specs, check_vma=False)
```

profile of v0, /device:TPU:4, one launch (start us, length us, event | category | flops | bytes accessed | tf_op | source)
XLA Modules:
  0.0 199.1 jit_solution(10223486780182810245)
XLA Ops:
  7.4 0.0 copy-start.2
  7.4 0.0 copy-start.1
  7.4 0.0 all-reduce.2.cloned.1.call-start
  7.4 2.5 %reduce_sum.9 = f32[2,16384]{1,0:T(2,128)} reduce(f32[10,2,16384]{2,1,0:T(2,128)} %param.7, f32[]{:T(128)} %constant.17.clone.1), dimensions={0}, to_apply=%region_0.1 | reduce | flops 294912 | bytes 1441796 | tf_op jit(solution)/shard_map/reduce_sum | solution.py:71
  9.9 0.0 all-reduce.2.cloned.1.call-update
  9.9 0.0 all-gather.2.cloned.1.call-start
  9.9 0.0 copy-done.2
  9.9 1.4 slice_reduce_fusion.1
  11.3 0.1 reshape_squeeze.9
  11.4 0.0 copy-done.1
  11.4 18.2 %cosine_reduce_fusion.1 = (f32[65536]{0:T(1024)S(1)}, f32[65536]{0:T(1024)S(1)}, f32[65536]{0:T(1024)S(1)}, f32[65536]{0:T(1024)S(1)}) fusion(f32[2,65536]{1,0:T(2,128)S(1)} %copy-done.1), kind=kLoop, calls=%fused_computation.12 | loop fusion | bytes 1572864 | tf_op jit(solution)/shard_map/cos | solution.py:8
  29.6 0.1 sin.47
  29.7 0.1 cos.40
  29.8 0.1 reshape_squeeze.8
  29.9 0.1 sin.45
  30.0 0.1 cos.42
  30.1 0.1 subtract_convert_fusion.1
  30.2 0.0 copy-start.3
  30.3 0.0 copy-start.4
  30.3 0.2 copy.33
  30.4 0.9 copy.35
  31.4 0.0 all-gather.2.cloned.1.call-update
  31.4 0.0 copy-done.3
  31.4 0.1 copy.39
  31.5 0.1 min.12
  31.6 0.1 copy.37
  31.7 0.1 copy.36
  31.8 0.1 copy.34
  31.9 0.1 sub.57
  32.0 1.7 gather_fusion
  33.7 0.1 copy.32
  33.9 0.0 copy-done.4
  33.9 0.1 iota_compare_fusion
  33.9 90.8 %all-reduce.2.cloned.1.call-done = f32[2,16384]{1,0:T(2,128)} async-done(((f32[2,16384]{1,0:T(2,128)}), f32[2,16384]{1,0:T(2,128)}) %all-reduce.2.cloned.1.call-update) | async-done | bytes 131088 | tf_op jit(solution)/shard_map/psum | solution.py:71
  124.7 1.0 broadcast_multiply_fusion
  125.7 23.8 %all-gather.2.cloned.1.call-done = bf16[8192,768]{1,0:T(8,128)(2,1)} async-done(((bf16[256,768]{1,0:T(8,128)(2,1)}), bf16[8192,768]{1,0:T(8,128)(2,1)}) %all-gather.2.cloned.1.call-update) | async-done | bytes 12582928 | tf_op jit(solution)/shard_map/all_gather | solution.py:50
  149.5 6.8 %gather_fusion.1 = bf16[32,768]{1,0:T(8,128)(2,1)S(1)} fusion(bf16[8192,768]{1,0:T(8,128)(2,1)} %all-gather.2.cloned.1.call-done, s32[1024]{0:T(1024)S(1)} %pad_clamp_fusion), kind=kCustom, calls=%fused_computation.1 | custom fusion | bytes 98432 | tf_op jit(solution)/shard_map/jit(_take)/gather | solution.py:53
  156.4 0.2 select_select_fusion
  156.6 0.0 copy-start
  156.6 3.0 %fusion.2 = f32[3,16,128]{2,0,1:T(4,128)S(1)} fusion(bf16[1,16,4,256,128]{4,3,2,1,0:T(8,128)(2,1)} %param.11, bf16[16,2,3,256]{3,2,1,0:T(4,128)(2,1)S(1)} %get-tuple-element.20, bf16[16,2,3,256]{3,2,1,0:T(4,128)(2,1)S(1)} %get-tuple-element.21, pred[16,4]{1,0:T(8,128)(4,1)S(1)} %iota_compare_fusion), kind=kOutput, calls=%fused_computation.5 | convolution fusion | flops 12828672 | bytes 4317248 | tf_op jit(solution)/shard_map/ikcf,ikfb->cib/dot_general | solution.py:64
  159.6 1.3 multiply_add_fusion
  160.9 29.1 %all_gather.7 = f32[2,16384]{1,0:T(2,128)S(1)} all-gather(f32[2,2048]{1,0:T(2,128)S(1)} %pad_maximum_fusion.1), channel_id=1, replica_groups=mesh['mem'=8,'tile'=32] {'mem'}, dimensions={1}, use_global_device_ids=true | all-gather | bytes 147456 | tf_op jit(solution)/shard_map/all_gather | solution.py:70
  190.0 0.0 copy-done
  190.0 1.6 subtract_add_fusion
  (10 shorter events, 0.2 us)
Async XLA Ops:
  7.4 2.6 %copy-start.2 = (f32[2,65536]{1,0:T(2,128)S(1)}, f32[2,65536]{1,0:T(2,128)}, u32[]{:S(2)}) copy-start(f32[2,65536]{1,0:T(2,128)} %param.8) | copy-start | bytes 1572868
  7.4 4.0 %copy-start.1 = (f32[2,65536]{1,0:T(2,128)S(1)}, f32[2,65536]{1,0:T(2,128)}, u32[]{:S(2)}) copy-start(f32[2,65536]{1,0:T(2,128)} %param.9) | copy-start | bytes 1572868
  7.4 117.3 %all-reduce.2.cloned.1.call-start = ((), (), s32[]{:S(2)}) async-start(), calls=%async_computation | async-start | bytes 262144 | tf_op jit(solution)/shard_map/psum | solution.py:71
  9.9 139.6 %all-gather.2.cloned.1.call-start = ((), (), s32[]{:S(2)}) async-start(), calls=%async_computation.1 | async-start | bytes 12976128 | tf_op jit(solution)/shard_map/all_gather | solution.py:50
  30.2 1.2 copy-start.3
  30.3 3.6 %copy-start.4 = (s32[1,16]{1,0:T(1,128)S(1)}, s32[1,16]{1,0:T(1,128)}, u32[]{:S(2)}) copy-start(s32[1,16]{1,0:T(1,128)} %param.13) | copy-start | bytes 196
  156.6 33.5 %copy-start = (f32[10,2,16384]{2,1,0:T(2,128)S(1)}, f32[10,2,16384]{2,1,0:T(2,128)}, u32[]{:S(2)}) copy-start(f32[10,2,16384]{2,1,0:T(2,128)} %param.7) | copy-start | bytes 3932164
Sparse Core Ops, SparseCore 0:
  10.8 113.8 all-reduce.1
Sparse Core Ops, SparseCore 1:
  31.5 118.0 all-gather.1
where the time goes:
time: 201 us; the launch traced here: 199 us
  waiting for transfers between devices  115 us (57%)
  local copies, waits for them, and re-layouts  30.4 us (15%)
  blocking collectives  29.1 us (14%)
  between operations  15.1 us (8%)
  other arithmetic  6.87 us (3%)
  matrix products  3.01 us (1%)
    psum x1, waiting for transfers between devices, shards(): member_total = lax.psum(jnp.sum(members, axis=0), 'mem')  90.8 us
    all_gather x1, blocking collectives, shards(): coarse_wind = lax.all_gather(own_wind, 'mem', axis=1, tiled=True)  29.1 us
    all_gather x1, waiting for transfers between devices, shards(): shard_piece = lax.all_gather(flat_blocks, 'tile', axis=0, tiled=True)  23.8 us
    cos x2, local copies, waits for them, and re-layouts, to_vector(): sin_lon, cos_lon = (jnp.sin(longitude), jnp.cos(longitude))  18.3 us
    gather x2, local copies, waits for them, and re-layouts, shards(): taken = jnp.take(shard_piece, jnp.clip(far_ids, 0, piece_rows - 1), axis=0)  6.87 us
  transfers between devices with their start and end apart: 2, of which 2 were waited for; matrix products, arithmetic and copies ran while one was open for 12% of the time, Pallas kernels for 0%

commit v1 on v0

v1 whole, which is shorter than its diff:
```python
import jax
import jax.numpy as jnp
from jax import lax
from jax.experimental import pallas as pl
from jax.experimental.pallas import tpu as pltpu
from jax.sharding import PartitionSpec as P

F32 = jnp.float32
BF16 = jnp.bfloat16
VMEM = pl.BlockSpec(memory_space=pltpu.VMEM)
SMEM = pl.BlockSpec(memory_space=pltpu.SMEM)
ANY = pl.BlockSpec(memory_space=pl.ANY)


def sin_cos(x):
    y = x * x
    s = F32(1.0 / 6227020800.0)
    for c in (-1.0 / 39916800.0, 1.0 / 362880.0, -1.0 / 5040.0, 1.0 / 120.0, -1.0 / 6.0):
        s = s * y + F32(c)
    c_ = F32(1.0 / 479001600.0)
    for c in (-1.0 / 3628800.0, 1.0 / 40320.0, -1.0 / 720.0, 1.0 / 24.0, -0.5):
        c_ = c_ * y + F32(c)
    return x + x * (y * s), F32(1.0) + y * c_


def flat(x):
    lead, columns = x.shape[:-2], x.shape[-1]
    chunks = columns // 128
    x = x.reshape(*lead, 2, chunks, 128)
    return jnp.swapaxes(x, -3, -2).reshape(*lead, 2 * chunks, 128)


def unflat(x):
    lead, rows = x.shape[:-2], x.shape[-2]
    x = x.reshape(*lead, rows // 2, 2, 128)
    return jnp.swapaxes(x, -3, -2).reshape(*lead, 2, rows * 64)


def sum_kernel(half_ref, members_ref, mine_ref, other_ref):
    rows = mine_ref.shape[0]
    half = half_ref[0]
    mine_ref[...] = jnp.sum(members_ref[:, pl.ds(pl.multiple_of(half * rows, rows), rows), :], axis=0)
    other_ref[...] = jnp.sum(members_ref[:, pl.ds(pl.multiple_of((1 - half) * rows, rows), rows), :], axis=0)


def add_kernel(y_ref, mine_ref, got_ref, own_ref, *send_refs):
    rows = own_ref.shape[0]
    y = y_ref[0]
    for k, ref in enumerate((own_ref,) + send_refs):
        at = pl.ds(pl.multiple_of((y ^ k) * rows, rows), rows)
        ref[...] = mine_ref[at, :] + got_ref[at, :]


def cart_kernel(inc_ref, ang_ref, cart_ref):
    step = 64

    def body(n, carry):
        at = pl.ds(pl.multiple_of(n * step, step), step)
        s, c = sin_cos(ang_ref[at, :].reshape(step // 8, 8, 128))
        u = inc_ref[at, :].reshape(step // 8, 8, 128)
        su, cu = s * u, c * u
        t = pltpu.roll(su, 7, 1)
        cart_ref[0, at, :] = (-su - c * t).reshape(step, 128)
        cart_ref[1, at, :] = (cu - s * t).reshape(step, 128)
        cart_ref[2, at, :] = pltpu.roll(cu, 7, 1).reshape(step, 128)
        return carry

    lax.fori_loop(0, inc_ref.shape[0] // step, body, 0)


def gather_kernel(where_ref, own_ref, r17_ref, r16_ref, rup_ref, cart_ref,
                  s17_ref, s16_ref, sup_ref, near_ref, own2_ref, tmp_ref):
    m = where_ref[0]
    blocks = own_ref.shape[1]
    fine = cart_ref.shape[1] // 4
    for n, (ids, slot, out) in enumerate(
        ((r17_ref, 3, s17_ref), (r16_ref, 3, s16_ref), (rup_ref, 2, sup_ref), (own_ref, 2, own2_ref))
    ):
        for i in range(blocks):
            row = 4 * (ids[slot, i] & (fine - 1))
            for c in range(3):
                tmp_ref[n, 3 * i + c : 3 * i + c + 1, 0:128] = cart_ref[c, pl.ds(row, 1), :]
                tmp_ref[n, 3 * i + c : 3 * i + c + 1, 128:256] = cart_ref[c, pl.ds(row + 2, 1), :]
        out[...] = tmp_ref[n].astype(BF16)
    first = pl.multiple_of(m * (blocks * 8), 8)
    for k in range(2):
        for c in range(3):
            for h in range(2):
                near_ref[2 * k + h, pl.ds(c, blocks, stride=3), :] = (
                    cart_ref[c, pl.ds(first + 4 * k + 2 * h, blocks, stride=8), :]
                )


def near_kernel(near_ref, weights_ref, acc_ref, held, sems):
    blocks = weights_ref.shape[0]
    copies = [
        pltpu.make_async_copy(weights_ref.at[i, pl.ds(0, 2)], held.at[i], sems.at[i]) for i in range(blocks)
    ]
    for copy in copies:
        copy.start()
    for i in range(blocks):
        lhs = jnp.concatenate([near_ref[n, 3 * i : 3 * i + 3, :] for n in range(4)], axis=1).astype(BF16)
        copies[i].wait()
        acc_ref[3 * i : 3 * i + 3, :] = jnp.dot(
            lhs, held[i].reshape(512, 128), preferred_element_type=F32
        )


def far_kernel(where_ref, ids_ref, counts_ref, acc_ref, own2_ref, gup_ref, g16_ref, g17_ref, ang_ref,
               p0_ref, p1_ref, p2_ref, p3_ref, weights_ref, delta_ref, rows, cart, wind, held, sems):
    blocks = weights_ref.shape[0]
    tile, fine_bits, sixteen, members = where_ref[1], 8, where_ref[2], F32(80.0)
    copies = [
        pltpu.make_async_copy(weights_ref.at[i, pl.ds(2, 2)], held.at[i], sems.at[i]) for i in range(blocks)
    ]
    for copy in copies:
        copy.start()
    for n, ref in enumerate((own2_ref, gup_ref, g16_ref, g17_ref)):
        rows[n] = ref[...].astype(F32)
    for i in range(blocks):
        at = slice(3 * i, 3 * i + 3)
        count = counts_ref[0, i]
        two = jnp.where((ids_ref[2, i] >> fine_bits) == tile, rows[0, at, :], rows[1, at, :])
        three = jnp.where((ids_ref[3, i] >> fine_bits) == sixteen, rows[2, at, :], rows[3, at, :])
        two = jnp.where(count > 2, two, 0.0)
        three = jnp.where(count > 3, three, 0.0)
        lhs = jnp.concatenate([two, three], axis=1).astype(BF16)
        copies[i].wait()
        cart[at, :] = acc_ref[at, :] + jnp.dot(lhs, held[i].reshape(512, 128), preferred_element_type=F32)
    x, y, z = (cart[pl.ds(c, blocks, stride=3), :] for c in range(3))
    sa, ca = sin_cos(ang_ref[pl.ds(0, blocks, stride=2), :])
    sp, cp = sin_cos(ang_ref[pl.ds(1, blocks, stride=2), :])
    wind[pl.ds(0, blocks, stride=2), :] = -sa * x + ca * y
    wind[pl.ds(1, blocks, stride=2), :] = -sp * ca * x - sp * sa * y + cp * z
    mean = (p0_ref[...] + p1_ref[...] + p2_ref[...] + p3_ref[...]) / members
    delta = wind[...] - mean
    for n in range(delta_ref.shape[0]):
        delta_ref[n] = delta


def out_kernel(members_ref, delta_ref, out_ref):
    out_ref[...] = members_ref[...] + delta_ref[...][None]


def shards(members, increment, fine_angles, coarse_angles, remap_weights, sources, counts):
    mems, tiles = lax.axis_size("mem"), lax.axis_size("tile")
    m, t = lax.axis_index("mem"), lax.axis_index("tile")
    weights = remap_weights[0]
    blocks = weights.shape[0]
    ids = sources[0].T
    flip = mems // 2
    far = tiles // 2

    def send(x, mem_flip, tile_shift):
        pairs = [
            (a * tiles + b, (a ^ mem_flip) * tiles + (b + tile_shift) % tiles)
            for a in range(mems)
            for b in range(tiles)
        ]
        return lax.ppermute(x, ("mem", "tile"), pairs)

    where = jnp.stack([m, t, (t + far) % tiles, m // 4, m % 4]).astype(jnp.int32)
    r17 = send(ids, flip, far + 1)
    r16 = send(ids, flip, far)
    rup = send(ids, 0, -1)

    members_rows = flat(members)
    total_rows = members_rows.shape[1]
    half = total_rows // 2
    piece = total_rows // mems
    row = lambda n, dtype=F32: jax.ShapeDtypeStruct((n, 128), dtype)
    mine, other = pl.pallas_call(
        sum_kernel, out_shape=(row(half), row(half)), in_specs=[SMEM, VMEM], out_specs=(VMEM, VMEM), name="member_sum"
    )((m // 4).reshape(1), members_rows)
    got = send(other, flip, 0)

    inc_rows, ang_rows = flat(increment), flat(fine_angles)
    cart = pl.pallas_call(
        cart_kernel,
        out_shape=jax.ShapeDtypeStruct((3,) + inc_rows.shape, F32),
        in_specs=[VMEM, VMEM],
        out_specs=VMEM,
        name="fine_cart",
    )(inc_rows, ang_rows)

    rows = jax.ShapeDtypeStruct((3 * blocks, 256), BF16)
    s17, s16, sup, near, own2 = pl.pallas_call(
        gather_kernel,
        out_shape=(rows, rows, rows, jax.ShapeDtypeStruct((4, 3 * blocks, 128), F32), rows),
        in_specs=[SMEM] * 5 + [VMEM],
        out_specs=(VMEM,) * 5,
        scratch_shapes=[pltpu.VMEM((4, 3 * blocks, 256), F32)],
        name="pick_rows",
    )(where, ids, r17, r16, rup, cart)
    g17 = send(s17, flip, -(far + 1))
    g16 = send(s16, flip, -far)
    gup = send(sup, 0, 1)

    p0, q1, q2, q3 = pl.pallas_call(
        add_kernel, out_shape=(row(piece),) * 4, in_specs=[SMEM, VMEM, VMEM], out_specs=(VMEM,) * 4, name="pair_sum"
    )((m % 4).reshape(1), mine, got)
    p1, p2, p3 = send(q1, 1, 0), send(q2, 2, 0), send(q3, 3, 0)

    acc = pl.pallas_call(
        near_kernel,
        out_shape=row(3 * blocks),
        in_specs=[VMEM, ANY],
        out_specs=VMEM,
        scratch_shapes=[pltpu.VMEM((blocks, 2, 256, 128), BF16), pltpu.SemaphoreType.DMA((blocks,))],
        name="near_slots",
    )(near, weights)

    angles = lax.dynamic_slice_in_dim(flat(coarse_angles), m * piece, piece, 0)
    delta = pl.pallas_call(
        far_kernel,
        out_shape=jax.ShapeDtypeStruct((mems, piece, 128), F32),
        in_specs=[SMEM] * 3 + [VMEM] * 10 + [ANY],
        out_specs=VMEM,
        scratch_shapes=[
            pltpu.VMEM((4, 3 * blocks, 256), F32),
            pltpu.VMEM((3 * blocks, 128), F32),
            pltpu.VMEM((piece, 128), F32),
            pltpu.VMEM((blocks, 2, 256, 128), BF16),
            pltpu.SemaphoreType.DMA((blocks,)),
        ],
        name="far_slots",
    )(where, ids, counts, acc, own2, gup, g16, g17, angles, p0, p1, p2, p3, weights)
    whole = lax.all_to_all(delta, "mem", 0, 0, tiled=True).reshape(total_rows, 128)
    return unflat(members_rows + whole[None])


def solution(mesh):
    in_specs = (
        P("mem", None, "tile"),
        P(None, "tile"),
        P(None, "tile"),
        P(None, "tile"),
        P("tile", "mem", None, None, None),
        P("tile", "mem", None),
        P("tile", "mem"),
    )
    out_specs = P("mem", None, "tile")
    return jax.shard_map(shards, mesh=mesh, in_specs=in_specs, out_specs=out_specs, check_vma=False)
```

time: 201 us -> 54.4 us (0.27)
  waiting for transfers between devices: 115 us -> 0.03 us
  local copies, waits for them, and re-layouts: 30.4 us -> 3.56 us
  starting transfers between devices: 0.05 us -> 19.2 us
  Pallas kernels: 0 us -> 18.5 us
  blocking collectives: 29.1 us -> 10.9 us
  between operations: 15.1 us -> 0.14 us
  other arithmetic: 6.87 us -> 1.6 us
  matrix products: 3.01 us -> 0 us
    psum x1 -> x0, waiting for transfers between devices: 90.8 us -> none  [shards(): member_total = lax.psum(jnp.sum(members, axis=0), 'mem')]
    all_gather x1 -> x0, blocking collectives: 29.1 us -> none  [shards(): coarse_wind = lax.all_gather(own_wind, 'mem', axis=1, tiled=True)]
    all_gather x1 -> x0, waiting for transfers between devices: 23.8 us -> none  [shards(): shard_piece = lax.all_gather(flat_blocks, 'tile', axis=0, tiled=True)]
    ppermute x0 -> x10, starting transfers between devices: none -> 19.2 us  [send(): return lax.ppermute(x, ('mem', 'tile'), pairs)]
    pallas_call x0 -> x6, Pallas kernels: none -> 18.5 us  [the longest x1 4.89 us: shards(): pl.pallas_call(far_kernel, out_shape=jax.ShapeDtypeStruct((mems, piece, 1...]
    cos x3 -> x0, local copies, waits for them, and re-layouts: 18.4 us -> none  [the longest x2 18.3 us: to_vector(): sin_lon, cos_lon = (jnp.sin(longitude), jnp.cos(longitude))]
    all_to_all x0 -> x1, blocking collectives: none -> 10.9 us  [shards(): lax.all_to_all(delta, 'mem', 0, 0, tiled=True).reshape(total_rows, 128)]
    gather x4 -> x0, local copies, waits for them, and re-layouts: 8.6 us -> none  [the longest x2 6.87 us: shards(): taken = jnp.take(shard_piece, jnp.clip(far_ids, 0, piece_rows - 1), axis=0)]
  transfers between devices with their start and end apart: 2 -> 10, of which waited for: 2 -> 0; matrix products, arithmetic and copies ran while one was open for 12% -> 2% of each run, Pallas kernels for 0% -> 21%
where the time goes in v1:
time: 54.4 us; the launch traced here: 53.9 us
  starting transfers between devices  19.2 us (35%)
  Pallas kernels  18.5 us (34%)
  blocking collectives  10.9 us (20%)
  local copies, waits for them, and re-layouts  3.56 us (7%)
  other arithmetic  1.6 us (3%)
    ppermute x10, starting transfers between devices, send(): return lax.ppermute(x, ('mem', 'tile'), pairs)  19.2 us
    all_to_all x1, blocking collectives, shards(): lax.all_to_all(delta, 'mem', 0, 0, tiled=True).reshape(total_rows, 128)  10.9 us
    pallas_call x1, Pallas kernels, shards(): pl.pallas_call(far_kernel, out_shape=jax.ShapeDtypeStruct((mems, piece, 1...  4.89 us
    pallas_call x1, Pallas kernels, shards(): pl.pallas_call(near_kernel, out_shape=row(3 * blocks), in_specs=[VMEM, AN...  4.72 us
    pallas_call x1, Pallas kernels, shards(): pl.pallas_call(cart_kernel, out_shape=jax.ShapeDtypeStruct((3,) + inc_row...  3.05 us
    unnamed x26, local copies, waits for them, and re-layouts  2.39 us
    pallas_call x1, Pallas kernels, shards(): pl.pallas_call(gather_kernel, out_shape=(rows, rows, rows, jax.ShapeDtype...  2.25 us
    pallas_call x1, Pallas kernels, shards(): pl.pallas_call(sum_kernel, out_shape=(row(half), row(half)), in_specs=[SM...  2.06 us
  transfers between devices with their start and end apart: 10, of which 0 were waited for; matrix products, arithmetic and copies ran while one was open for 2% of the time, Pallas kernels for 21%

profile of v1, /device:TPU:4, one launch (start us, length us, event | category | flops | bytes accessed | tf_op | source)
XLA Modules:
  0.0 53.9 jit_solution(15190407326030318471)
XLA Ops:
  0.0 0.0 copy-start
  0.0 2.1 %member_sum.1 = (f32[128,128]{1,0:T(8,128)}, f32[128,128]{1,0:T(8,128)}) custom-call(s32[1]{0:T(128)} %bitcast.3.half_ref, f32[10,256,128]{2,1,0:T(8,128)} %bitcast.37), custom_call_target="tpu_custom_call" | custom-call | tf_op jit(solution)/shard_map/member_sum/pallas_call | solution.py:172
  2.1 1.2 %collective-permute-start.6 = (f32[128,128]{1,0:T(8,128)}, f32[128,128]{1,0:T(8,128)S(1)}, u32[]{:S(2)}, u32[]{:S(2)}) collective-permute-start(f32[128,128]{1,0:T(8,128)} %get-tuple-element.22), channel_id=1, source_target_pairs={{0,128},{1,129},{2,130},{3,131},{4,132},{5,133},{6,134},{7,135},{8... | collective-permute-start | bytes 196616 | tf_op jit(solution)/shard_map/ppermute | solution.py:160
  3.3 0.0 copy-done.9
  3.3 0.0 collective-permute-start
  3.3 1.6 %collective-permute-start.1 = (s32[4,16]{1,0:T(4,128)S(1)}, s32[4,16]{1,0:T(4,128)S(1)}, u32[]{:S(2)}, u32[]{:S(2)}) collective-permute-start(s32[4,16]{1,0:T(4,128)S(1)} %bitcast.44), channel_id=1, source_target_pairs={{0,144},{1,145},{2,146},{3,147},{4,148},{5,149},{6,150},{7,151},{8... | collective-permute-start | bytes 776 | tf_op jit(solution)/shard_map/ppermute | solution.py:160
  4.9 5.5 %collective-permute-start.2 = (s32[4,16]{1,0:T(4,128)S(1)}, s32[4,16]{1,0:T(4,128)S(1)}, u32[]{:S(2)}, u32[]{:S(2)}) collective-permute-start(s32[4,16]{1,0:T(4,128)S(1)} %bitcast.45), channel_id=1, source_target_pairs={{0,31},{1,0},{2,1},{3,2},{4,3},{5,4},{6,5},{7,6},{8,7},{9,8},{10,9... | collective-permute-start | bytes 776 | tf_op jit(solution)/shard_map/ppermute | solution.py:160
  10.4 3.1 %fine_cart.1.cart_ref = f32[3,1024,128]{2,1,0:T(8,128)} custom-call(f32[1024,128]{1,0:T(8,128)} %bitcast.38, f32[1024,128]{1,0:T(8,128)} %bitcast.39), custom_call_target="tpu_custom_call" | custom-call | tf_op jit(solution)/shard_map/fine_cart/pallas_call | solution.py:178
  13.4 0.6 %stack.23.where_ref = s32[5]{0:T(128)} concatenate(s32[1]{0:T(128)} %bitcast, s32[1]{0:T(128)} %bitcast.1, s32[1]{0:T(128)} %bitcast.2, s32[1]{0:T(128)} %bitcast.3.half_ref, s32[1]{0:T(128)} %bitcast.4.y_ref), dimensions={0} | concatenate | bytes 40 | tf_op jit(solution)/shard_map/stack | solution.py:162
  14.0 0.0 collective-permute-done.r17_ref
  14.0 0.0 collective-permute-done.1.r16_ref
  14.0 0.0 copy-start.11
  14.0 0.0 collective-permute-done.2.rup_ref
  14.0 0.6 %copy-done.10 = s32[4,16]{1,0:T(4,128)} copy-done((s32[4,16]{1,0:T(4,128)}, s32[4,16]{1,0:T(4,128)S(1)}, u32[]{:S(2)}) %copy-start.10) | copy-done | bytes 280
  14.6 0.0 copy-done.11
  14.6 0.6 %copy-done.12 = s32[4,16]{1,0:T(4,128)} copy-done((s32[4,16]{1,0:T(4,128)}, s32[4,16]{1,0:T(4,128)S(1)}, u32[]{:S(2)}) %copy-start.12) | copy-done | bytes 280
  15.2 2.2 %pick_rows.1 = (bf16[48,256]{1,0:T(8,128)(2,1)}, bf16[48,256]{1,0:T(8,128)(2,1)}, bf16[48,256]{1,0:T(8,128)(2,1)}, f32[4,48,128]{2,1,0:T(8,128)}, bf16[48,256]{1,0:T(8,128)(2,1)}) custom-call(s32[5]{0:T(128)} %stack.23.where_ref, s32[4,16]{1,0:T(4,128)} %bitcast.41, s32[4,16]{1,0:T(4,128)} %copy-done.10, s32[4,16]{1,0:T(4,128)} %copy-done.11, ...), custom_call_target="tpu_custom_call" | custom-call | tf_op jit(solution)/shard_map/pick_rows/pallas_call | solution.py:187
  17.4 0.0 collective-permute-start.3
  17.4 0.6 %collective-permute-start.4 = (bf16[48,256]{1,0:T(8,128)(2,1)}, bf16[48,256]{1,0:T(8,128)(2,1)S(1)}, u32[]{:S(2)}, u32[]{:S(2)}) collective-permute-start(bf16[48,256]{1,0:T(8,128)(2,1)} %get-tuple-element.19), channel_id=1, source_target_pairs={{0,144},{1,145},{2,146},{3,147},{4,148},{5,149},{6,150},{7,151},{8... | collective-permute-start | bytes 73736 | tf_op jit(solution)/shard_map/ppermute | solution.py:160
  18.0 5.6 %collective-permute-start.5 = (bf16[48,256]{1,0:T(8,128)(2,1)}, bf16[48,256]{1,0:T(8,128)(2,1)S(1)}, u32[]{:S(2)}, u32[]{:S(2)}) collective-permute-start(bf16[48,256]{1,0:T(8,128)(2,1)} %get-tuple-element.20), channel_id=1, source_target_pairs={{0,143},{1,144},{2,145},{3,146},{4,147},{5,148},{6,149},{7,150},{8... | collective-permute-start | bytes 73736 | tf_op jit(solution)/shard_map/ppermute | solution.py:160
  23.7 0.0 collective-permute-done.6.got_ref
  23.7 0.6 %copy-done.2 = f32[128,128]{1,0:T(8,128)} copy-done((f32[128,128]{1,0:T(8,128)}, f32[128,128]{1,0:T(8,128)S(1)}, u32[]{:S(2)}) %copy-start.2) | copy-done | bytes 65560
  24.3 1.5 %pair_sum.1 = (f32[32,128]{1,0:T(8,128)}, f32[32,128]{1,0:T(8,128)}, f32[32,128]{1,0:T(8,128)}, f32[32,128]{1,0:T(8,128)}) custom-call(s32[1]{0:T(128)} %bitcast.4.y_ref, f32[128,128]{1,0:T(8,128)} %get-tuple-element.21.mine_ref, f32[128,128]{1,0:T(8,128)} %copy-done.2), custom_call_target="tpu_custom_call" | custom-call | tf_op jit(solution)/shard_map/pair_sum/pallas_call | solution.py:199
  25.8 1.6 %collective-permute-start.7 = (f32[32,128]{1,0:T(8,128)}, f32[32,128]{1,0:T(8,128)S(1)}, u32[]{:S(2)}, u32[]{:S(2)}) collective-permute-start(f32[32,128]{1,0:T(8,128)} %get-tuple-element.24), channel_id=1, source_target_pairs={{0,32},{1,33},{2,34},{3,35},{4,36},{5,37},{6,38},{7,39},{8,40},{9,... | collective-permute-start | bytes 49160 | tf_op jit(solution)/shard_map/ppermute | solution.py:160
  27.4 2.9 %collective-permute-start.8 = (f32[32,128]{1,0:T(8,128)}, f32[32,128]{1,0:T(8,128)S(1)}, u32[]{:S(2)}, u32[]{:S(2)}) collective-permute-start(f32[32,128]{1,0:T(8,128)} %get-tuple-element.25), channel_id=1, source_target_pairs={{0,64},{1,65},{2,66},{3,67},{4,68},{5,69},{6,70},{7,71},{8,72},{9,... | collective-permute-start | bytes 49160 | tf_op jit(solution)/shard_map/ppermute | solution.py:160
  30.3 0.0 collective-permute-done.3.gup_ref
  30.3 0.2 collective-permute-start.9
  30.5 0.0 copy-done
  30.5 0.6 %constant_dynamic-slice_fusion.ang_ref = f32[32,128]{1,0:T(8,128)} fusion(f32[256,128]{1,0:T(8,128)S(1)} %bitcast.34, s32[]{:T(128)S(6)} %select_n.24), kind=kLoop, calls=%fused_computation.1 | loop fusion | bytes 32772 | tf_op jit(solution)/shard_map/dynamic_slice | solution.py:213
  31.1 4.7 %near_slots.1.acc_ref = f32[48,128]{1,0:T(8,128)} custom-call(f32[4,48,128]{2,1,0:T(8,128)} %get-tuple-element.16.near_ref, bf16[16,4,256,128]{3,2,1,0:T(8,128)(2,1)} %bitcast.35), custom_call_target="tpu_custom_call" | custom-call | tf_op jit(solution)/shard_map/near_slots/pallas_call | solution.py:204
  35.9 0.0 copy-done.3
  35.9 0.0 collective-permute-done.4.g16_ref
  35.9 0.0 copy-start.4
  35.9 0.0 collective-permute-done.5.g17_ref
  35.9 0.0 copy-start.5
  35.9 0.0 collective-permute-done.7.p1_ref
  35.9 0.0 copy-start.6
  35.9 0.0 collective-permute-done.8.p2_ref
  35.9 0.0 copy-start.7
  35.9 0.0 collective-permute-done.9.p3_ref
  36.0 0.5 copy-done.4
  36.5 0.0 copy-done.5
  36.5 0.0 copy-done.6
  36.5 0.0 copy-done.7
  36.5 0.0 copy-done.8
  36.6 4.9 %far_slots.1 = f32[8,32,128]{2,1,0:T(8,128)} custom-call(s32[5]{0:T(128)} %stack.23.where_ref, s32[4,16]{1,0:T(4,128)} %bitcast.42, s32[1,16]{1,0:T(1,128)} %counts_ref.1, f32[48,128]{1,0:T(8,128)} %near_slots.1.acc_ref, bf16[48,256]{1,0:T(8,128)(2,1)} %get-tuple-element.17.own2_ref, bf16[48,256]{1,0:T(8,128)(2,1)} %copy-done.3, bf16[48,256]{1,0:T(8,128)(2,1)} %copy-done.4, ...), custom_call_target="tpu_custom_call" | custom-call | tf_op jit(solution)/shard_map/far_slots/pallas_call | solution.py:214
  41.5 10.9 %all_to_all.5 = f32[8,32,128]{2,1,0:T(8,128)S(1)} all-to-all(f32[8,32,128]{2,1,0:T(8,128)} %far_slots.1), channel_id=1, replica_groups=mesh['mem'=8,'tile'=32] {'mem'}, dimensions={0} | all-to-all | bytes 262144 | tf_op jit(solution)/shard_map/all_to_all | solution.py:228
  52.4 1.6 %broadcast_add_fusion = f32[10,2,16384]{2,1,0:T(2,128)} fusion(f32[10,2,16384]{2,1,0:T(2,128)S(1)} %copy-done.1, f32[2,16384]{1,0:T(2,128)S(1)} %bitcast.40), kind=kLoop, calls=%fused_computation | loop fusion | flops 327680 | bytes 2752512 | tf_op jit(solution)/shard_map/add | solution.py:229
  (8 shorter events, 0.0 us)
Async XLA Ops:
  0.0 30.5 %copy-start = (f32[2,16384]{1,0:T(2,128)S(1)}, f32[2,16384]{1,0:T(2,128)}, u32[]{:S(2)}) copy-start(f32[2,16384]{1,0:T(2,128)} %param.10) | copy-start | bytes 393220
  0.0 3.3 %copy-start.9 = (s32[1,16,4]{1,2,0:T(4,128)S(1)}, s32[1,16,4]{1,2,0:T(4,128)}, u32[]{:S(2)}) copy-start(s32[1,16,4]{1,2,0:T(4,128)} %param.12) | copy-start | bytes 772
  2.1 21.6 %collective-permute-start.6 = (f32[128,128]{1,0:T(8,128)}, f32[128,128]{1,0:T(8,128)S(1)}, u32[]{:S(2)}, u32[]{:S(2)}) collective-permute-start(f32[128,128]{1,0:T(8,128)} %get-tuple-element.22), channel_id=1, source_target_pairs={{0,128},{1,129},{2,130},{3,131},{4,132},{5,133},{6,134},{7,135},{8... | collective-permute-start | bytes 196616 | tf_op jit(solution)/shard_map/ppermute | solution.py:160
  3.3 10.7 %collective-permute-start = (s32[4,16]{1,0:T(4,128)S(1)}, s32[4,16]{1,0:T(4,128)S(1)}, u32[]{:S(2)}, u32[]{:S(2)}) collective-permute-start(s32[4,16]{1,0:T(4,128)S(1)} %bitcast.43), channel_id=1, source_target_pairs={{0,145},{1,146},{2,147},{3,148},{4,149},{5,150},{6,151},{7,152},{8... | collective-permute-start | bytes 776 | tf_op jit(solution)/shard_map/ppermute | solution.py:160
  3.3 10.7 %collective-permute-start.1 = (s32[4,16]{1,0:T(4,128)S(1)}, s32[4,16]{1,0:T(4,128)S(1)}, u32[]{:S(2)}, u32[]{:S(2)}) collective-permute-start(s32[4,16]{1,0:T(4,128)S(1)} %bitcast.44), channel_id=1, source_target_pairs={{0,144},{1,145},{2,146},{3,147},{4,148},{5,149},{6,150},{7,151},{8... | collective-permute-start | bytes 776 | tf_op jit(solution)/shard_map/ppermute | solution.py:160
  4.9 9.1 %collective-permute-start.2 = (s32[4,16]{1,0:T(4,128)S(1)}, s32[4,16]{1,0:T(4,128)S(1)}, u32[]{:S(2)}, u32[]{:S(2)}) collective-permute-start(s32[4,16]{1,0:T(4,128)S(1)} %bitcast.45), channel_id=1, source_target_pairs={{0,31},{1,0},{2,1},{3,2},{4,3},{5,4},{6,5},{7,6},{8,7},{9,8},{10,9... | collective-permute-start | bytes 776 | tf_op jit(solution)/shard_map/ppermute | solution.py:160
  14.0 0.6 %copy-start.10 = (s32[4,16]{1,0:T(4,128)}, s32[4,16]{1,0:T(4,128)S(1)}, u32[]{:S(2)}) copy-start(s32[4,16]{1,0:T(4,128)S(1)} %collective-permute-done.r17_ref) | copy-start | bytes 772
  14.0 0.6 %copy-start.11 = (s32[4,16]{1,0:T(4,128)}, s32[4,16]{1,0:T(4,128)S(1)}, u32[]{:S(2)}) copy-start(s32[4,16]{1,0:T(4,128)S(1)} %collective-permute-done.1.r16_ref) | copy-start | bytes 772
  14.6 0.6 %copy-start.12 = (s32[4,16]{1,0:T(4,128)}, s32[4,16]{1,0:T(4,128)S(1)}, u32[]{:S(2)}) copy-start(s32[4,16]{1,0:T(4,128)S(1)} %collective-permute-done.2.rup_ref) | copy-start | bytes 772
  17.4 12.9 %collective-permute-start.3 = (bf16[48,256]{1,0:T(8,128)(2,1)}, bf16[48,256]{1,0:T(8,128)(2,1)S(1)}, u32[]{:S(2)}, u32[]{:S(2)}) collective-permute-start(bf16[48,256]{1,0:T(8,128)(2,1)} %get-tuple-element.18), channel_id=1, source_target_pairs={{0,1},{1,2},{2,3},{3,4},{4,5},{5,6},{6,7},{7,8},{8,9},{9,10},{10,1... | collective-permute-start | bytes 73736 | tf_op jit(solution)/shard_map/ppermute | solution.py:160
  17.4 18.4 %collective-permute-start.4 = (bf16[48,256]{1,0:T(8,128)(2,1)}, bf16[48,256]{1,0:T(8,128)(2,1)S(1)}, u32[]{:S(2)}, u32[]{:S(2)}) collective-permute-start(bf16[48,256]{1,0:T(8,128)(2,1)} %get-tuple-element.19), channel_id=1, source_target_pairs={{0,144},{1,145},{2,146},{3,147},{4,148},{5,149},{6,150},{7,151},{8... | collective-permute-start | bytes 73736 | tf_op jit(solution)/shard_map/ppermute | solution.py:160
  18.0 17.8 %collective-permute-start.5 = (bf16[48,256]{1,0:T(8,128)(2,1)}, bf16[48,256]{1,0:T(8,128)(2,1)S(1)}, u32[]{:S(2)}, u32[]{:S(2)}) collective-permute-start(bf16[48,256]{1,0:T(8,128)(2,1)} %get-tuple-element.20), channel_id=1, source_target_pairs={{0,143},{1,144},{2,145},{3,146},{4,147},{5,148},{6,149},{7,150},{8... | collective-permute-start | bytes 73736 | tf_op jit(solution)/shard_map/ppermute | solution.py:160
  23.7 0.6 %copy-start.2 = (f32[128,128]{1,0:T(8,128)}, f32[128,128]{1,0:T(8,128)S(1)}, u32[]{:S(2)}) copy-start(f32[128,128]{1,0:T(8,128)S(1)} %collective-permute-done.6.got_ref) | copy-start | bytes 196612
  25.8 10.1 %collective-permute-start.7 = (f32[32,128]{1,0:T(8,128)}, f32[32,128]{1,0:T(8,128)S(1)}, u32[]{:S(2)}, u32[]{:S(2)}) collective-permute-start(f32[32,128]{1,0:T(8,128)} %get-tuple-element.24), channel_id=1, source_target_pairs={{0,32},{1,33},{2,34},{3,35},{4,36},{5,37},{6,38},{7,39},{8,40},{9,... | collective-permute-start | bytes 49160 | tf_op jit(solution)/shard_map/ppermute | solution.py:160
  27.4 8.5 %collective-permute-start.8 = (f32[32,128]{1,0:T(8,128)}, f32[32,128]{1,0:T(8,128)S(1)}, u32[]{:S(2)}, u32[]{:S(2)}) collective-permute-start(f32[32,128]{1,0:T(8,128)} %get-tuple-element.25), channel_id=1, source_target_pairs={{0,64},{1,65},{2,66},{3,67},{4,68},{5,69},{6,70},{7,71},{8,72},{9,... | collective-permute-start | bytes 49160 | tf_op jit(solution)/shard_map/ppermute | solution.py:160
  30.3 5.6 %copy-start.3 = (bf16[48,256]{1,0:T(8,128)(2,1)}, bf16[48,256]{1,0:T(8,128)(2,1)S(1)}, u32[]{:S(2)}) copy-start(bf16[48,256]{1,0:T(8,128)(2,1)S(1)} %collective-permute-done.3.gup_ref) | copy-start | bytes 73732
  30.3 5.6 %collective-permute-start.9 = (f32[32,128]{1,0:T(8,128)}, f32[32,128]{1,0:T(8,128)S(1)}, u32[]{:S(2)}, u32[]{:S(2)}) collective-permute-start(f32[32,128]{1,0:T(8,128)} %get-tuple-element.26), channel_id=1, source_target_pairs={{0,96},{1,97},{2,98},{3,99},{4,100},{5,101},{6,102},{7,103},{8,104... | collective-permute-start | bytes 49160 | tf_op jit(solution)/shard_map/ppermute | solution.py:160
  35.9 0.6 %copy-start.4 = (bf16[48,256]{1,0:T(8,128)(2,1)}, bf16[48,256]{1,0:T(8,128)(2,1)S(1)}, u32[]{:S(2)}) copy-start(bf16[48,256]{1,0:T(8,128)(2,1)S(1)} %collective-permute-done.4.g16_ref) | copy-start | bytes 73732
  35.9 0.6 %copy-start.5 = (bf16[48,256]{1,0:T(8,128)(2,1)}, bf16[48,256]{1,0:T(8,128)(2,1)S(1)}, u32[]{:S(2)}) copy-start(bf16[48,256]{1,0:T(8,128)(2,1)S(1)} %collective-permute-done.5.g17_ref) | copy-start | bytes 73732
  35.9 0.6 %copy-start.6 = (f32[32,128]{1,0:T(8,128)}, f32[32,128]{1,0:T(8,128)S(1)}, u32[]{:S(2)}) copy-start(f32[32,128]{1,0:T(8,128)S(1)} %collective-permute-done.7.p1_ref) | copy-start | bytes 49156
  35.9 0.6 %copy-start.7 = (f32[32,128]{1,0:T(8,128)}, f32[32,128]{1,0:T(8,128)S(1)}, u32[]{:S(2)}) copy-start(f32[32,128]{1,0:T(8,128)S(1)} %collective-permute-done.8.p2_ref) | copy-start | bytes 49156
  36.0 0.6 %copy-start.8 = (f32[32,128]{1,0:T(8,128)}, f32[32,128]{1,0:T(8,128)S(1)}, u32[]{:S(2)}) copy-start(f32[32,128]{1,0:T(8,128)S(1)} %collective-permute-done.9.p3_ref) | copy-start | bytes 49156
  36.6 15.8 %copy-start.1 = (f32[10,2,16384]{2,1,0:T(2,128)S(1)}, f32[10,2,16384]{2,1,0:T(2,128)}, u32[]{:S(2)}) copy-start(f32[10,2,16384]{2,1,0:T(2,128)} %param.7) | copy-start | bytes 3932164

commit v2 on v0

v2 whole, which is shorter than its diff:
```python
import jax
import jax.numpy as jnp
from jax import lax
from jax.experimental import pallas as pl
from jax.experimental.pallas import tpu as pltpu
from jax.sharding import PartitionSpec as P

F32 = jnp.float32
BF16 = jnp.bfloat16
VMEM = pl.BlockSpec(memory_space=pltpu.VMEM)
SMEM = pl.BlockSpec(memory_space=pltpu.SMEM)
ANY = pl.BlockSpec(memory_space=pl.ANY)
HBM = pl.BlockSpec(memory_space=pltpu.HBM)


def placed(x, spec):
    if spec is VMEM:
        return pltpu.with_memory_space_constraint(x, pltpu.VMEM)
    return pltpu.with_memory_space_constraint(x, pltpu.HBM) if spec is HBM else x


def split(index, count, rows):
    return pl.ds(pl.multiple_of(index * rows, rows), rows)


def sin_cos(x):
    y = x * x
    s = F32(1.0 / 6227020800.0)
    for c in (-1.0 / 39916800.0, 1.0 / 362880.0, -1.0 / 5040.0, 1.0 / 120.0, -1.0 / 6.0):
        s = s * y + F32(c)
    c_ = F32(1.0 / 479001600.0)
    for c in (-1.0 / 3628800.0, 1.0 / 40320.0, -1.0 / 720.0, 1.0 / 24.0, -0.5):
        c_ = c_ * y + F32(c)
    return x + x * (y * s), F32(1.0) + y * c_


def flat(x):
    lead, columns = x.shape[:-2], x.shape[-1]
    chunks = columns // 128
    x = x.reshape(*lead, 2, chunks, 128)
    return jnp.swapaxes(x, -3, -2).reshape(*lead, 2 * chunks, 128)


def unflat(x):
    lead, rows = x.shape[:-2], x.shape[-2]
    x = x.reshape(*lead, rows // 2, 2, 128)
    return jnp.swapaxes(x, -3, -2).reshape(*lead, 2, rows * 64)


def pair_kernel(mine_ref, got_ref, after_ref, keep_ref, send_ref):
    del after_ref
    rows = keep_ref.shape[0]
    half = lax.rem(lax.axis_index("mem"), 2)
    for ref, part in ((keep_ref, half), (send_ref, 1 - half)):
        at = split(part, 2, rows)
        ref[...] = mine_ref[at, :] + got_ref[at, :]


def cart_kernel(inc_hbm, ang_hbm, cart_ref, even_ref, inc, ang, sems):
    parts = sems.shape[0]
    step = inc.shape[0] // parts
    loads = [
        [pltpu.make_async_copy(src.at[split(n, parts, step)], dst.at[split(n, parts, step)], sems.at[n, k])
         for k, (src, dst) in enumerate(((inc_hbm, inc), (ang_hbm, ang)))]
        for n in range(parts)
    ]
    for pair in loads:
        for load in pair:
            load.start()
    for n in range(parts):
        for load in loads[n]:
            load.wait()

        def body(k, carry, n=n):
            rows = 64
            at = pl.ds(pl.multiple_of(n * step + k * rows, rows), rows)
            s, c = sin_cos(ang[at, :].reshape(rows // 8, 8, 128))
            u = inc[at, :].reshape(rows // 8, 8, 128)
            su, cu = s * u, c * u
            t = pltpu.roll(su, 7, 1)
            cart_ref[0, at, :] = (-su - c * t).reshape(rows, 128)
            cart_ref[1, at, :] = (cu - s * t).reshape(rows, 128)
            cart_ref[2, at, :] = pltpu.roll(cu, 7, 1).reshape(rows, 128)
            return carry

        lax.fori_loop(0, step // 64, body, 0)
        half = step // 2
        for c in range(3):
            even_ref[c, n * half : (n + 1) * half, :] = cart_ref[c, pl.ds(n * step, half, stride=2), :].astype(BF16)


def sum_kernel(members_hbm, after_ref, members_ref, keep_ref, send_ref, sems):
    del after_ref
    count, rows = members_hbm.shape[0], keep_ref.shape[0]
    half = lax.axis_index("mem") // 4
    loads = [
        [pltpu.make_async_copy(members_hbm.at[n, split(h, 2, rows)], members_ref.at[n, split(h, 2, rows)], sems.at[n, k])
         for n in range(count)]
        for k, h in enumerate((1 - half, half))
    ]
    for part in loads:
        for load in part:
            load.start()
    for part, h, ref in ((loads[0], 1 - half, send_ref), (loads[1], half, keep_ref)):
        for load in part:
            load.wait()
        ref[...] = jnp.sum(members_ref[:, split(h, 2, rows), :], axis=0)


def pick_kernel(r17_ref, r16_ref, cart_ref, s17_ref, s16_ref, ids, tmp, sems):
    fine = cart_ref.shape[1] // 4
    asked = ((r17_ref, s17_ref), (r16_ref, s16_ref))
    copies = [pltpu.make_async_copy(ref, ids.at[n], sems.at[n]) for n, (ref, _) in enumerate(asked)]
    for copy in copies:
        copy.start()
    for copy in copies:
        copy.wait()
    for n, (ref, out) in enumerate(asked):
        for i in range(ref.shape[1]):
            row = 4 * (ids[n, 3, i] & (fine - 1))
            for c in range(3):
                for h in range(2):
                    tmp[n, 3 * i + c : 3 * i + c + 1, 128 * h : 128 * h + 128] = (
                        cart_ref[c, pl.ds(row + 2 * h, 1), :]
                    )
        out[...] = tmp[n].astype(BF16)


def near_kernel(ids_ref, counts_ref, cart_ref, below_ref, weights_ref, acc_ref, m16_ref, m17_ref, near, below):
    blocks = weights_ref.shape[0]
    fine = cart_ref.shape[1] // 4
    tiles = lax.axis_size("tile")
    tile = lax.axis_index("tile")
    across = lax.rem(tile + tiles // 2, tiles)
    first = pl.multiple_of(lax.axis_index("mem") * (blocks * 8), 8)
    below[...] = below_ref[...].astype(F32)
    for k in range(2):
        for c in range(3):
            for h in range(2):
                near[2 * k + h, pl.ds(c, blocks, stride=3), :] = (
                    cart_ref[c, pl.ds(first + 4 * k + 2 * h, blocks, stride=8), :]
                )
    for i in range(blocks):
        count, two, three = counts_ref[0, i], ids_ref[2, i], ids_ref[3, i]
        row, mine = two & (fine - 1), two // fine == tile
        for c in range(3):
            for h in range(2):
                got = jnp.where(mine, cart_ref[c, pl.ds(4 * row + 2 * h, 1), :], below[c, pl.ds(2 * row + h, 1), :])
                near[4 + h, 3 * i + c : 3 * i + c + 1, :] = jnp.where(count > 2, got, 0.0)
        at = slice(3 * i, 3 * i + 3)
        flag = lambda yes: jnp.full((3, 128), jnp.where(yes, F32(1.0), F32(0.0)))
        m16_ref[at, :] = flag((count > 3) & (three // fine == across))
        m17_ref[at, :] = flag((count > 3) & (three // fine != across))
    for i in range(blocks):
        at = slice(3 * i, 3 * i + 3)
        lhs = jnp.concatenate([near[n, at, :] for n in range(6)], axis=1).astype(BF16)
        acc_ref[at, :] = jnp.dot(lhs, weights_ref[i, 0:3].reshape(768, 128), preferred_element_type=F32)


def far_kernel(acc_ref, m16_ref, m17_ref, g16_ref, g17_ref, ang_ref, keep_ref, got_ref, weights_ref,
               out_ref, three, cart, wind):
    blocks, piece = weights_ref.shape[0], wind.shape[0]
    wide = lambda ref: jnp.concatenate([ref[...], ref[...]], axis=1) > 0.5
    three[...] = jnp.where(
        wide(m16_ref), g16_ref[...].astype(F32), jnp.where(wide(m17_ref), g17_ref[...].astype(F32), 0.0)
    )
    for i in range(blocks):
        at = slice(3 * i, 3 * i + 3)
        cart[at, :] = acc_ref[at, :] + jnp.dot(
            three[at, :].astype(BF16), weights_ref[i, 3], preferred_element_type=F32
        )
    x, y, z = (cart[pl.ds(c, blocks, stride=3), :] for c in range(3))
    first = lax.axis_index("mem") * piece
    sa, ca = sin_cos(ang_ref[pl.ds(first, blocks, stride=2), :])
    sp, cp = sin_cos(ang_ref[pl.ds(first + 1, blocks, stride=2), :])
    wind[pl.ds(0, blocks, stride=2), :] = -sa * x + ca * y
    wind[pl.ds(1, blocks, stride=2), :] = -sp * ca * x - sp * sa * y + cp * z
    total = keep_ref[...] + got_ref[...]
    for n in range(out_ref.shape[0]):
        out_ref[n, 0:piece, :] = wind[...]
        out_ref[n, piece:, :] = total


def out_kernel(members_ref, all_ref, out_ref, delta, buffer, sems):
    piece = delta.shape[0] // all_ref.shape[0]
    for h in range(2):
        for b in range(2):
            mean = (all_ref[4 * h + b, piece:, :] + all_ref[4 * h + b + 2, piece:, :]) / F32(80.0)
            first = 4 * h + 2 * b
            for n in range(2):
                at = slice((first + n) * piece, (first + n + 1) * piece)
                delta[at, :] = all_ref[first + n, 0:piece, :] - mean[n * piece : (n + 1) * piece, :]
    count = members_ref.shape[0]
    copies = [pltpu.make_async_copy(buffer.at[i], out_ref.at[i], sems.at[i]) for i in range(count)]
    for i in range(count):
        buffer[i] = members_ref[i] + delta[...]
        copies[i].start()
    for copy in copies:
        copy.wait()


def call(kernel, name, outs, specs, scratch=(), out_space=pltpu.VMEM, cost=1.0):
    shapes = tuple(out_space(shape, dtype) for shape, dtype in outs)
    out_specs = tuple(pl.BlockSpec(memory_space=out_space) for _ in outs)

    def run(*args):
        args = [placed(x, spec) for x, spec in zip(args, specs, strict=True)]
        return pl.pallas_call(
            kernel, out_shape=shapes, in_specs=specs, out_specs=out_specs, scratch_shapes=list(scratch), name=name,
            cost_estimate=pl.CostEstimate(flops=int(cost * 1e9), bytes_accessed=int(cost * 3.6e6), transcendentals=0),
            compiler_params=pltpu.CompilerParams(vmem_limit_bytes=8 * 2**20),
        )(*args)

    return run


def shards(members, increment, fine_angles, coarse_angles, remap_weights, sources, counts):
    mems, tiles = lax.axis_size("mem"), lax.axis_size("tile")
    weights = remap_weights[0]
    blocks = weights.shape[0]
    ids = sources[0].T
    flip = mems // 2
    far = tiles // 2

    def send(x, mem_flip, tile_shift):
        pairs = [
            (a * tiles + b, (a ^ mem_flip) * tiles + (b + tile_shift) % tiles)
            for a in range(mems)
            for b in range(tiles)
        ]
        return lax.ppermute(x, ("mem", "tile"), pairs)

    r17 = send(ids, flip, far + 1)
    r16 = send(ids, flip, far)

    inc_rows, ang_rows = flat(increment), flat(fine_angles)
    fine_rows = inc_rows.shape[0]
    cart, even = call(
        cart_kernel,
        "fine_cart",
        [((3, fine_rows, 128), F32), ((3, fine_rows // 2, 128), BF16)],
        [HBM, HBM],
        [pltpu.VMEM(inc_rows.shape, F32)] * 2 + [pltpu.SemaphoreType.DMA((4, 2))],
        cost=20,
    )(inc_rows, ang_rows)
    below = send(even, 0, 1)

    members_rows = flat(members)
    count, total_rows = members_rows.shape[:2]
    piece = total_rows // mems
    row = lambda n, dtype=F32: ((n, 128), dtype)
    members_rows, mine, other = call(
        sum_kernel,
        "member_sum",
        [(members_rows.shape, F32)] + [row(4 * piece)] * 2,
        [HBM, ANY],
        [pltpu.SemaphoreType.DMA((count, 2))],
        cost=20,
    )(members_rows, cart)
    got = send(other, flip, 0)

    rows = ((3 * blocks, 256), BF16)
    s17, s16 = call(
        pick_kernel,
        "pick_rows",
        [rows] * 2,
        [VMEM] * 3,
        [pltpu.SMEM((2,) + ids.shape, jnp.int32), pltpu.VMEM((2, 3 * blocks, 256), F32), pltpu.SemaphoreType.DMA((2,))],
        cost=20,
    )(r17, r16, cart)
    g17 = send(s17, flip, -(far + 1))
    g16 = send(s16, flip, -far)

    keep, other = call(pair_kernel, "pair_sum", [row(2 * piece)] * 2, [VMEM, VMEM, ANY])(mine, got, s17)
    got = send(other, 1, 0)

    near = call(
        near_kernel,
        "near_slots",
        [row(3 * blocks)] * 3,
        [SMEM, SMEM, VMEM, VMEM, VMEM],
        [pltpu.VMEM((6, 3 * blocks, 128), F32), pltpu.VMEM((3, fine_rows // 2, 128), F32)],
        cost=20,
    )(ids, counts, cart, below, weights)

    (payload,) = call(
        far_kernel,
        "far_slots",
        [((mems, 3 * piece, 128), F32)],
        [VMEM] * 9,
        [pltpu.VMEM((3 * blocks, 256), F32), pltpu.VMEM((3 * blocks, 128), F32), pltpu.VMEM((piece, 128), F32)],
    )(*near, g16, g17, flat(coarse_angles), keep, got, weights)
    payload = lax.all_to_all(payload, "mem", 0, 0, tiled=True)
    (out,) = call(
        out_kernel,
        "recentre",
        [(members_rows.shape, F32)],
        [VMEM, VMEM],
        [pltpu.VMEM((total_rows, 128), F32), pltpu.VMEM(members_rows.shape, F32), pltpu.SemaphoreType.DMA((count,))],
        pltpu.HBM,
    )(members_rows, payload)
    return unflat(out)


def solution(mesh):
    in_specs = (
        P("mem", None, "tile"),
        P(None, "tile"),
        P(None, "tile"),
        P(None, "tile"),
        P("tile", "mem", None, None, None),
        P("tile", "mem", None),
        P("tile", "mem"),
    )
    out_specs = P("mem", None, "tile")
    return jax.shard_map(shards, mesh=mesh, in_specs=in_specs, out_specs=out_specs, check_vma=False)
```

time: 201 us -> 33.8 us (0.17)
  the two profiles are of different devices: /device:TPU:4 before, /device:TPU:97 now
where the time goes in v2:
time: 33.8 us; the launch traced here: 33.5 us
  blocking collectives  12.6 us (37%)
  starting transfers between devices  11.3 us (33%)
  Pallas kernels  6.66 us (20%)
  waiting for transfers between devices  2.85 us (8%)
    all_to_all x1, blocking collectives, shards(): payload = lax.all_to_all(payload, 'mem', 0, 0, tiled=True)  12.6 us
    ppermute x7, starting transfers between devices, send(): return lax.ppermute(x, ('mem', 'tile'), pairs)  11.3 us
    pallas_call x7, Pallas kernels, run(): pl.pallas_call(kernel, out_shape=shapes, in_specs=specs, out_specs=out_sp...  6.66 us
    ppermute x7, waiting for transfers between devices, send(): return lax.ppermute(x, ('mem', 'tile'), pairs)  2.85 us
  transfers between devices with their start and end apart: 7, of which 1 were waited for; matrix products, arithmetic and copies ran while one was open for 0% of the time, Pallas kernels for 16%

profile of v2, /device:TPU:97, one launch (start us, length us, event | category | flops | bytes accessed | tf_op | source)
XLA Modules:
  0.0 33.5 jit_solution(18156590352854119942)
XLA Ops:
  0.0 2.5 %collective-permute-start.2 = (s32[4,16]{1,0:T(4,128)}, s32[4,16]{1,0:T(4,128)S(1)}, u32[]{:S(2)}, u32[]{:S(2)}) collective-permute-start(s32[4,16]{1,0:T(4,128)} %bitcast.32), channel_id=1, source_target_pairs={{0,144},{1,145},{2,146},{3,147},{4,148},{5,149},{6,150},{7,151},{8... | collective-permute-start | bytes 776 | tf_op jit(solution)/shard_map/ppermute | solution.py:231
  2.5 3.6 %collective-permute-start.1 = (s32[4,16]{1,0:T(4,128)}, s32[4,16]{1,0:T(4,128)S(1)}, u32[]{:S(2)}, u32[]{:S(2)}) collective-permute-start(s32[4,16]{1,0:T(4,128)} %bitcast.33), channel_id=1, source_target_pairs={{0,145},{1,146},{2,147},{3,148},{4,149},{5,150},{6,151},{7,152},{8... | collective-permute-start | bytes 776 | tf_op jit(solution)/shard_map/ppermute | solution.py:231
  6.1 1.8 %fine_cart.1 = (f32[3,1024,128]{2,1,0:T(8,128)S(1)}, bf16[3,512,128]{2,1,0:T(8,128)(2,1)S(1)}) custom-call(f32[1024,128]{1,0:T(8,128)} %bitcast.36, f32[1024,128]{1,0:T(8,128)} %bitcast.37), custom_call_target="tpu_custom_call" | custom-call | flops 20000000000 | bytes 72000000 | tf_op jit(solution)/shard_map/fine_cart/pallas_call | solution.py:208
  7.9 0.2 collective-permute-start
  8.0 1.5 %member_sum.1 = (f32[10,256,128]{2,1,0:T(8,128)S(1)}, f32[128,128]{1,0:T(8,128)S(1)}, f32[128,128]{1,0:T(8,128)S(1)}) custom-call(f32[10,256,128]{2,1,0:T(8,128)} %bitcast.35, f32[3,1024,128]{2,1,0:T(8,128)S(1)} %get-tuple-element.17.after_ref.cart_ref), custom_call_target="tpu_custom_call" | custom-call | flops 20000000000 | bytes 72000000 | tf_op jit(solution)/shard_map/member_sum/pallas_call | solution.py:208
  9.6 0.1 collective-permute-start.5
  9.7 0.0 collective-permute-done.2.r16_ref
  9.7 0.0 collective-permute-done.1.r17_ref
  9.7 0.0 copy-start
  9.7 0.7 %pick_rows.1 = (bf16[48,256]{1,0:T(8,128)(2,1)S(1)}, bf16[48,256]{1,0:T(8,128)(2,1)S(1)}) custom-call(s32[4,16]{1,0:T(4,128)S(1)} %collective-permute-done.1.r17_ref, s32[4,16]{1,0:T(4,128)S(1)} %collective-permute-done.2.r16_ref, f32[3,1024,128]{2,1,0:T(8,128)S(1)} %get-tuple-element.17.after_ref.cart_ref), custom_call_target="tpu_custom_call" | custom-call | flops 20000000000 | bytes 72000000 | tf_op jit(solution)/shard_map/pick_rows/pallas_call | solution.py:208
  10.4 2.5 %collective-permute-start.3 = (bf16[48,256]{1,0:T(8,128)(2,1)S(1)}, bf16[48,256]{1,0:T(8,128)(2,1)S(1)}, u32[]{:S(2)}, u32[]{:S(2)}) collective-permute-start(bf16[48,256]{1,0:T(8,128)(2,1)S(1)} %get-tuple-element.23), channel_id=1, source_target_pairs={{0,144},{1,145},{2,146},{3,147},{4,148},{5,149},{6,150},{7,151},{8... | collective-permute-start | bytes 73736 | tf_op jit(solution)/shard_map/ppermute | solution.py:231
  12.9 1.1 %collective-permute-start.4 = (bf16[48,256]{1,0:T(8,128)(2,1)S(1)}, bf16[48,256]{1,0:T(8,128)(2,1)S(1)}, u32[]{:S(2)}, u32[]{:S(2)}) collective-permute-start(bf16[48,256]{1,0:T(8,128)(2,1)S(1)} %get-tuple-element.24.after_ref), channel_id=1, source_target_pairs={{0,143},{1,144},{2,145},{3,146},{4,147},{5,148},{6,149},{7,150},{8... | collective-permute-start | bytes 73736 | tf_op jit(solution)/shard_map/ppermute | solution.py:231
  14.0 0.0 collective-permute-done.5.got_ref
  14.0 0.0 copy-start.2
  14.0 0.0 copy-start.3
  14.0 1.4 %collective-permute-start.6 = (f32[64,128]{1,0:T(8,128)S(1)}, f32[64,128]{1,0:T(8,128)S(1)}, u32[]{:S(2)}, u32[]{:S(2)}) collective-permute-start(f32[64,128]{1,0:T(8,128)S(1)} %get-tuple-element.28), channel_id=1, source_target_pairs={{0,32},{1,33},{2,34},{3,35},{4,36},{5,37},{6,38},{7,39},{8,40},{9,... | collective-permute-start | bytes 98312 | tf_op jit(solution)/shard_map/ppermute | solution.py:231
  15.4 0.0 collective-permute-done.below_ref
  15.4 0.0 copy-done
  15.4 0.0 copy-done.2
  15.4 0.0 copy-done.3
  15.4 0.0 copy-start.1
  15.5 1.2 %near_slots.1 = (f32[48,128]{1,0:T(8,128)S(1)}, f32[48,128]{1,0:T(8,128)S(1)}, f32[48,128]{1,0:T(8,128)S(1)}) custom-call(s32[4,16]{1,0:T(4,128)S(1)} %bitcast.34, s32[1,16]{1,0:T(1,128)S(1)} %copy-done.3, f32[3,1024,128]{2,1,0:T(8,128)S(1)} %get-tuple-element.17.after_ref.cart_ref, bf16[3,512,128]{2,1,0:T(8,128)(2,1)S(1)} %collective-permute-done.below_ref, ...), custom_call_target="tpu_custom_call" | custom-call | flops 20000000000 | bytes 72000000 | tf_op jit(solution)/shard_map/near_slots/pallas_call | solution.py:208
  16.7 0.0 collective-permute-done.3.g16_ref
  16.7 2.8 %collective-permute-done.4.g17_ref = bf16[48,256]{1,0:T(8,128)(2,1)S(1)} collective-permute-done((bf16[48,256]{1,0:T(8,128)(2,1)S(1)}, bf16[48,256]{1,0:T(8,128)(2,1)S(1)}, u32[]{:S(2)}, u32[]{:S(2)}) %collective-permute-start.4) | collective-permute-done | bytes 24608 | tf_op jit(solution)/shard_map/ppermute | solution.py:231
  19.5 0.0 collective-permute-done.6.got_ref
  19.5 0.0 copy-done.1
  19.5 0.3 far_slots.1
  19.8 12.6 %all_to_all.5.all_ref = f32[8,96,128]{2,1,0:T(8,128)S(1)} all-to-all(f32[8,96,128]{2,1,0:T(8,128)S(1)} %far_slots.1), channel_id=1, replica_groups=mesh['mem'=8,'tile'=32] {'mem'}, dimensions={0} | all-to-all | bytes 786432 | tf_op jit(solution)/shard_map/all_to_all | solution.py:293
  32.4 1.2 %recentre.1 = f32[10,256,128]{2,1,0:T(8,128)} custom-call(f32[10,256,128]{2,1,0:T(8,128)S(1)} %get-tuple-element.18.members_ref, f32[8,96,128]{2,1,0:T(8,128)S(1)} %all_to_all.5.all_ref), custom_call_target="tpu_custom_call" | custom-call | flops 1000000000 | bytes 3600000 | tf_op jit(solution)/shard_map/recentre/pallas_call | solution.py:208
  (1 shorter events, 0.0 us)
Async XLA Ops:
  0.0 9.7 %collective-permute-start.2 = (s32[4,16]{1,0:T(4,128)}, s32[4,16]{1,0:T(4,128)S(1)}, u32[]{:S(2)}, u32[]{:S(2)}) collective-permute-start(s32[4,16]{1,0:T(4,128)} %bitcast.32), channel_id=1, source_target_pairs={{0,144},{1,145},{2,146},{3,147},{4,148},{5,149},{6,150},{7,151},{8... | collective-permute-start | bytes 776 | tf_op jit(solution)/shard_map/ppermute | solution.py:231
  2.5 7.2 %collective-permute-start.1 = (s32[4,16]{1,0:T(4,128)}, s32[4,16]{1,0:T(4,128)S(1)}, u32[]{:S(2)}, u32[]{:S(2)}) collective-permute-start(s32[4,16]{1,0:T(4,128)} %bitcast.33), channel_id=1, source_target_pairs={{0,145},{1,146},{2,147},{3,148},{4,149},{5,150},{6,151},{7,152},{8... | collective-permute-start | bytes 776 | tf_op jit(solution)/shard_map/ppermute | solution.py:231
  7.9 7.6 %collective-permute-start = (bf16[3,512,128]{2,1,0:T(8,128)(2,1)S(1)}, bf16[3,512,128]{2,1,0:T(8,128)(2,1)S(1)}, u32[]{:S(2)}, u32[]{:S(2)}) collective-permute-start(bf16[3,512,128]{2,1,0:T(8,128)(2,1)S(1)} %get-tuple-element.19), channel_id=1, source_target_pairs={{0,1},{1,2},{2,3},{3,4},{4,5},{5,6},{6,7},{7,8},{8,9},{9,10},{10,1... | collective-permute-start | bytes 1179656 | tf_op jit(solution)/shard_map/ppermute | solution.py:231
  9.6 4.5 %collective-permute-start.5 = (f32[128,128]{1,0:T(8,128)S(1)}, f32[128,128]{1,0:T(8,128)S(1)}, u32[]{:S(2)}, u32[]{:S(2)}) collective-permute-start(f32[128,128]{1,0:T(8,128)S(1)} %get-tuple-element.26), channel_id=1, source_target_pairs={{0,128},{1,129},{2,130},{3,131},{4,132},{5,133},{6,134},{7,135},{8... | collective-permute-start | bytes 196616 | tf_op jit(solution)/shard_map/ppermute | solution.py:231
  9.7 5.7 %copy-start = (bf16[1,16,4,256,128]{4,3,2,1,0:T(8,128)(2,1)S(1)}, bf16[1,16,4,256,128]{4,3,2,1,0:T(8,128)(2,1)}, u32[]{:S(2)}) copy-start(bf16[1,16,4,256,128]{4,3,2,1,0:T(8,128)(2,1)} %param.11) | copy-start | bytes 12582916
  10.4 6.2 %collective-permute-start.3 = (bf16[48,256]{1,0:T(8,128)(2,1)S(1)}, bf16[48,256]{1,0:T(8,128)(2,1)S(1)}, u32[]{:S(2)}, u32[]{:S(2)}) collective-permute-start(bf16[48,256]{1,0:T(8,128)(2,1)S(1)} %get-tuple-element.23), channel_id=1, source_target_pairs={{0,144},{1,145},{2,146},{3,147},{4,148},{5,149},{6,150},{7,151},{8... | collective-permute-start | bytes 73736 | tf_op jit(solution)/shard_map/ppermute | solution.py:231
  12.9 6.6 %collective-permute-start.4 = (bf16[48,256]{1,0:T(8,128)(2,1)S(1)}, bf16[48,256]{1,0:T(8,128)(2,1)S(1)}, u32[]{:S(2)}, u32[]{:S(2)}) collective-permute-start(bf16[48,256]{1,0:T(8,128)(2,1)S(1)} %get-tuple-element.24.after_ref), channel_id=1, source_target_pairs={{0,143},{1,144},{2,145},{3,146},{4,147},{5,148},{6,149},{7,150},{8... | collective-permute-start | bytes 73736 | tf_op jit(solution)/shard_map/ppermute | solution.py:231
  14.0 1.4 %copy-start.2 = (s32[1,16,4]{1,2,0:T(4,128)S(1)}, s32[1,16,4]{1,2,0:T(4,128)}, u32[]{:S(2)}) copy-start(s32[1,16,4]{1,2,0:T(4,128)} %param.12) | copy-start | bytes 772
  14.0 1.4 %copy-start.3 = (s32[1,16]{1,0:T(1,128)S(1)}, s32[1,16]{1,0:T(1,128)}, u32[]{:S(2)}) copy-start(s32[1,16]{1,0:T(1,128)} %counts_ref.1) | copy-start | bytes 196
  14.0 5.5 %collective-permute-start.6 = (f32[64,128]{1,0:T(8,128)S(1)}, f32[64,128]{1,0:T(8,128)S(1)}, u32[]{:S(2)}, u32[]{:S(2)}) collective-permute-start(f32[64,128]{1,0:T(8,128)S(1)} %get-tuple-element.28), channel_id=1, source_target_pairs={{0,32},{1,33},{2,34},{3,35},{4,36},{5,37},{6,38},{7,39},{8,40},{9,... | collective-permute-start | bytes 98312 | tf_op jit(solution)/shard_map/ppermute | solution.py:231
  15.4 4.1 %copy-start.1 = (f32[2,16384]{1,0:T(2,128)S(1)}, f32[2,16384]{1,0:T(2,128)}, u32[]{:S(2)}) copy-start(f32[2,16384]{1,0:T(2,128)} %param.10) | copy-start | bytes 393220

commit v3 on v2

--- a/solution.py
+++ b/solution.py
@@ -89,85 +89,120 @@
             even_ref[c, n * half : (n + 1) * half, :] = cart_ref[c, pl.ds(n * step, half, stride=2), :].astype(BF16)
 
 
-def sum_kernel(members_hbm, after_ref, members_ref, keep_ref, send_ref, sems):
+def first_kernel(inc_hbm, ang_hbm, members_hbm, cart_ref, even_ref, members_ref, inc, ang, odd, sems, member_sems):
+    parts, count = sems.shape[0], members_hbm.shape[0]
+    step = inc.shape[0] // parts
+    loads = [
+        [pltpu.make_async_copy(src.at[split(n, parts, step)], dst.at[split(n, parts, step)], sems.at[n, k])
+         for k, (src, dst) in enumerate(((inc_hbm, inc), (ang_hbm, ang)))]
+        for n in range(parts)
+    ]
+    member_loads = [
+        pltpu.make_async_copy(members_hbm.at[n], members_ref.at[n], member_sems.at[n]) for n in range(count)
+    ]
+    for load in sum(loads, []) + member_loads:
+        load.start()
+    for n in range(parts):
+        for load in loads[n]:
+            load.wait()
+
+        def body(k, carry, n=n):
+            rows = 64
+            at = pl.ds(pl.multiple_of(n * step + k * rows, rows), rows)
+            s, c = sin_cos(ang[at, :].reshape(rows // 8, 8, 128))
+            u = inc[at, :].reshape(rows // 8, 8, 128)
+            su, cu = s * u, c * u
+            t = pltpu.roll(su, 7, 1)
+            odd[0, at, :] = (-su - c * t).reshape(rows, 128)
+            odd[1, at, :] = (cu - s * t).reshape(rows, 128)
+            odd[2, at, :] = pltpu.roll(cu, 7, 1).reshape(rows, 128)
+            return carry
+
+        lax.fori_loop(0, step // 64, body, 0)
+        half = step // 2
+        for c in range(3):
+            kept = odd[c, pl.ds(n * step, half, stride=2), :]
+            cart_ref[c, n * half : (n + 1) * half, :] = kept
+            even_ref[c, n * half : (n + 1) * half, :] = kept.astype(BF16)
+    for load in member_loads:
+        load.wait()
+
+
+def sum_kernel(members_ref, keep_ref, send_ref):
+    rows = keep_ref.shape[0]
+    half = lax.axis_index("mem") // 4
+    keep_ref[...] = jnp.sum(members_ref[:, split(half, 2, rows), :], axis=0)
+    send_ref[...] = jnp.sum(members_ref[:, split(1 - half, 2, rows), :], axis=0)
+
+
+def pair_kernel(mine_ref, got_ref, after_ref, keep_ref, send_ref):
     del after_ref
-    count, rows = members_hbm.shape[0], keep_ref.shape[0]
-    half = lax.axis_index("mem") // 4
-    loads = [
-        [pltpu.make_async_copy(members_hbm.at[n, split(h, 2, rows)], members_ref.at[n, split(h, 2, rows)], sems.at[n, k])
-         for n in range(count)]
-        for k, h in enumerate((1 - half, half))
-    ]
-    for part in loads:
-        for load in part:
-            load.start()
-    for part, h, ref in ((loads[0], 1 - half, send_ref), (loads[1], half, keep_ref)):
-        for load in part:
-            load.wait()
-        ref[...] = jnp.sum(members_ref[:, split(h, 2, rows), :], axis=0)
+    rows = keep_ref.shape[0]
+    half = lax.rem(lax.axis_index("mem"), 2)
+    for ref, part in ((keep_ref, half), (send_ref, 1 - half)):
+        at = split(part, 2, rows)
+        ref[...] = mine_ref[at, :] + got_ref[at, :]
 
 
 def pick_kernel(r17_ref, r16_ref, cart_ref, s17_ref, s16_ref, ids, tmp, sems):
-    fine = cart_ref.shape[1] // 4
-    asked = ((r17_ref, s17_ref), (r16_ref, s16_ref))
-    copies = [pltpu.make_async_copy(ref, ids.at[n], sems.at[n]) for n, (ref, _) in enumerate(asked)]
+    fine = cart_ref.shape[1] // 2
+    asked = ((r17_ref, 3, s17_ref), (r16_ref, 3, s16_ref))
+    copies = [pltpu.make_async_copy(ref, ids.at[n], sems.at[n]) for n, (ref, _, _) in enumerate(asked)]
     for copy in copies:
         copy.start()
     for copy in copies:
         copy.wait()
-    for n, (ref, out) in enumerate(asked):
+    for n, (ref, slot, out) in enumerate(asked):
         for i in range(ref.shape[1]):
-            row = 4 * (ids[n, 3, i] & (fine - 1))
+            row = 2 * (ids[n, slot, i] & (fine - 1))
             for c in range(3):
                 for h in range(2):
-                    tmp[n, 3 * i + c : 3 * i + c + 1, 128 * h : 128 * h + 128] = (
-                        cart_ref[c, pl.ds(row + 2 * h, 1), :]
-                    )
+                    tmp[n, 3 * i + c : 3 * i + c + 1, 128 * h : 128 * h + 128] = cart_ref[c, pl.ds(row + h, 1), :]
         out[...] = tmp[n].astype(BF16)
 
 
-def near_kernel(ids_ref, counts_ref, cart_ref, below_ref, weights_ref, acc_ref, m16_ref, m17_ref, near, below):
+def near_kernel(ids_ref, counts_ref, cart_ref, below_ref, weights_ref, acc_ref, m17_ref, m16_ref, near, below):
     blocks = weights_ref.shape[0]
-    fine = cart_ref.shape[1] // 4
+    fine = cart_ref.shape[1] // 2
     tiles = lax.axis_size("tile")
     tile = lax.axis_index("tile")
     across = lax.rem(tile + tiles // 2, tiles)
-    first = pl.multiple_of(lax.axis_index("mem") * (blocks * 8), 8)
+    first = pl.multiple_of(lax.axis_index("mem") * (blocks * 4), 8)
     below[...] = below_ref[...].astype(F32)
     for k in range(2):
         for c in range(3):
             for h in range(2):
                 near[2 * k + h, pl.ds(c, blocks, stride=3), :] = (
-                    cart_ref[c, pl.ds(first + 4 * k + 2 * h, blocks, stride=8), :]
+                    cart_ref[c, pl.ds(first + 2 * k + h, blocks, stride=4), :]
                 )
     for i in range(blocks):
         count, two, three = counts_ref[0, i], ids_ref[2, i], ids_ref[3, i]
-        row, mine = two & (fine - 1), two // fine == tile
+        row, mine, straight = 2 * (two & (fine - 1)), two // fine == tile, three // fine == across
         for c in range(3):
             for h in range(2):
-                got = jnp.where(mine, cart_ref[c, pl.ds(4 * row + 2 * h, 1), :], below[c, pl.ds(2 * row + h, 1), :])
+                got = jnp.where(mine, cart_ref[c, pl.ds(row + h, 1), :], below[c, pl.ds(row + h, 1), :])
                 near[4 + h, 3 * i + c : 3 * i + c + 1, :] = jnp.where(count > 2, got, 0.0)
         at = slice(3 * i, 3 * i + 3)
         flag = lambda yes: jnp.full((3, 128), jnp.where(yes, F32(1.0), F32(0.0)))
-        m16_ref[at, :] = flag((count > 3) & (three // fine == across))
-        m17_ref[at, :] = flag((count > 3) & (three // fine != across))
+        m17_ref[at, :] = flag((count > 3) & ~straight)
+        m16_ref[at, :] = flag((count > 3) & straight)
     for i in range(blocks):
         at = slice(3 * i, 3 * i + 3)
         lhs = jnp.concatenate([near[n, at, :] for n in range(6)], axis=1).astype(BF16)
         acc_ref[at, :] = jnp.dot(lhs, weights_ref[i, 0:3].reshape(768, 128), preferred_element_type=F32)
 
 
-def far_kernel(acc_ref, m16_ref, m17_ref, g16_ref, g17_ref, ang_ref, keep_ref, got_ref, weights_ref,
-               out_ref, three, cart, wind):
+def far_kernel(acc_ref, m17_ref, m16_ref, g17_ref, g16_ref, ang_ref, keep_ref, got_ref, weights_ref,
+               out_ref, rows, cart, wind):
     blocks, piece = weights_ref.shape[0], wind.shape[0]
     wide = lambda ref: jnp.concatenate([ref[...], ref[...]], axis=1) > 0.5
-    three[...] = jnp.where(
+    rows[...] = jnp.where(
         wide(m16_ref), g16_ref[...].astype(F32), jnp.where(wide(m17_ref), g17_ref[...].astype(F32), 0.0)
     )
     for i in range(blocks):
         at = slice(3 * i, 3 * i + 3)
         cart[at, :] = acc_ref[at, :] + jnp.dot(
-            three[at, :].astype(BF16), weights_ref[i, 3], preferred_element_type=F32
+            rows[at, :].astype(BF16), weights_ref[i, 3], preferred_element_type=F32
         )
     x, y, z = (cart[pl.ds(c, blocks, stride=3), :] for c in range(3))
     first = lax.axis_index("mem") * piece
@@ -230,33 +265,38 @@
         ]
         return lax.ppermute(x, ("mem", "tile"), pairs)
 
-    r17 = send(ids, flip, far + 1)
-    r16 = send(ids, flip, far)
-
-    inc_rows, ang_rows = flat(increment), flat(fine_angles)
+    def shifted(shift):
+        pairs = []
+        for a in range(mems):
+            for b in range(tiles):
+                c = (b + shift) % tiles
+                near = a ^ flip if b // far != c // far else a
+                pairs.append((a * tiles + b, near * tiles + c))
+        return pairs
+
+    axes = ("mem", "tile")
+    p17, p16 = shifted(far + 1), shifted(far)
+    r17, r16 = (lax.ppermute(ids, axes, p) for p in (p17, p16))
+
+    inc_rows, ang_rows, members_rows = flat(increment), flat(fine_angles), flat(members)
     fine_rows = inc_rows.shape[0]
-    cart, even = call(
-        cart_kernel,
-        "fine_cart",
-        [((3, fine_rows, 128), F32), ((3, fine_rows // 2, 128), BF16)],
-        [HBM, HBM],
-        [pltpu.VMEM(inc_rows.shape, F32)] * 2 + [pltpu.SemaphoreType.DMA((4, 2))],
-        cost=20,
-    )(inc_rows, ang_rows)
-    below = send(even, 0, 1)
-
-    members_rows = flat(members)
     count, total_rows = members_rows.shape[:2]
     piece = total_rows // mems
     row = lambda n, dtype=F32: ((n, 128), dtype)
-    members_rows, mine, other = call(
-        sum_kernel,
-        "member_sum",
-        [(members_rows.shape, F32)] + [row(4 * piece)] * 2,
-        [HBM, ANY],
-        [pltpu.SemaphoreType.DMA((count, 2))],
+    whole = (3, fine_rows // 2, 128)
+    cart, even, members_rows = call(
+        first_kernel,
+        "fine_cart",
+        [(whole, F32), (whole, BF16), (members_rows.shape, F32)],
+        [HBM] * 3,
+        [pltpu.VMEM(inc_rows.shape, F32)] * 2
+        + [pltpu.VMEM((3, fine_rows, 128), F32), pltpu.SemaphoreType.DMA((4, 2)), pltpu.SemaphoreType.DMA((count,))],
         cost=20,
-    )(members_rows, cart)
+    )(inc_rows, ang_rows, members_rows)
+
+    below = lax.ppermute(even, axes, shifted(1))
+
+    mine, other = call(sum_kernel, "member_sum", [row(4 * piece)] * 2, [VMEM], cost=20)(members_rows)
     got = send(other, flip, 0)
 
     rows = ((3 * blocks, 256), BF16)
@@ -268,8 +308,7 @@
         [pltpu.SMEM((2,) + ids.shape, jnp.int32), pltpu.VMEM((2, 3 * blocks, 256), F32), pltpu.SemaphoreType.DMA((2,))],
         cost=20,
     )(r17, r16, cart)
-    g17 = send(s17, flip, -(far + 1))
-    g16 = send(s16, flip, -far)
+    g17, g16 = (lax.ppermute(x, axes, [(d, a) for a, d in p]) for x, p in ((s17, p17), (s16, p16)))
 
     keep, other = call(pair_kernel, "pair_sum", [row(2 * piece)] * 2, [VMEM, VMEM, ANY])(mine, got, s17)
     got = send(other, 1, 0)
@@ -279,7 +318,7 @@
         "near_slots",
         [row(3 * blocks)] * 3,
         [SMEM, SMEM, VMEM, VMEM, VMEM],
-        [pltpu.VMEM((6, 3 * blocks, 128), F32), pltpu.VMEM((3, fine_rows // 2, 128), F32)],
+        [pltpu.VMEM((6, 3 * blocks, 128), F32), pltpu.VMEM(whole, F32)],
         cost=20,
     )(ids, counts, cart, below, weights)
 
@@ -289,7 +328,7 @@
         [((mems, 3 * piece, 128), F32)],
         [VMEM] * 9,
         [pltpu.VMEM((3 * blocks, 256), F32), pltpu.VMEM((3 * blocks, 128), F32), pltpu.VMEM((piece, 128), F32)],
-    )(*near, g16, g17, flat(coarse_angles), keep, got, weights)
+    )(*near, g17, g16, flat(coarse_angles), keep, got, weights)
     payload = lax.all_to_all(payload, "mem", 0, 0, tiled=True)
     (out,) = call(
         out_kernel,

time: 33.8 us -> 32.4 us (0.959)
  Pallas kernels: 6.66 us -> 5.55 us
    ppermute x7 -> x2, starting transfers between devices: 11.3 us -> 1.47 us  [send(): return lax.ppermute(x, ('mem', 'tile'), pairs)]
    ppermute x0 -> x5, starting transfers between devices: none -> 9.6 us  [the longest x2 6.08 us: shards(): r17, r16 = (lax.ppermute(ids, axes, p) for p in (p17, p16))]
    ppermute x0 -> x5, waiting for transfers between devices: none -> 3.08 us  [the longest x2 3.07 us: shards(): lax.ppermute(x, axes, [(d, a) for a, d in p])]
    ppermute x7 -> x2, waiting for transfers between devices: 2.85 us -> 0.01 us  [send(): return lax.ppermute(x, ('mem', 'tile'), pairs)]
    pallas_call x7, Pallas kernels: 6.66 us -> 5.55 us  [run(): pl.pallas_call(kernel, out_shape=shapes, in_specs=specs, out_specs=out_sp...]
  transfers between devices with their start and end apart: 7 -> 7, of which waited for: 1 -> 1; matrix products, arithmetic and copies ran while one was open for 0% -> 0% of each run, Pallas kernels for 16% -> 13%
where the time goes in v3:
time: 32.4 us; the launch traced here: 32.2 us
  blocking collectives  12.4 us (38%)
  starting transfers between devices  11.1 us (34%)
  Pallas kernels  5.55 us (17%)
  waiting for transfers between devices  3.08 us (10%)
    all_to_all x1, blocking collectives, shards(): payload = lax.all_to_all(payload, 'mem', 0, 0, tiled=True)  12.4 us
    ppermute x2, starting transfers between devices, shards(): r17, r16 = (lax.ppermute(ids, axes, p) for p in (p17, p16))  6.08 us
    pallas_call x7, Pallas kernels, run(): pl.pallas_call(kernel, out_shape=shapes, in_specs=specs, out_specs=out_sp...  5.55 us
    ppermute x2, starting transfers between devices, shards(): lax.ppermute(x, axes, [(d, a) for a, d in p])  3.21 us
    ppermute x2, waiting for transfers between devices, shards(): lax.ppermute(x, axes, [(d, a) for a, d in p])  3.07 us
    ppermute x2, starting transfers between devices, send(): return lax.ppermute(x, ('mem', 'tile'), pairs)  1.47 us
  transfers between devices with their start and end apart: 7, of which 1 were waited for; matrix products, arithmetic and copies ran while one was open for 0% of the time, Pallas kernels for 13%

profile of v3, /device:TPU:97, one launch (start us, length us, event | category | flops | bytes accessed | tf_op | source)
XLA Modules:
  0.0 32.2 jit_solution(8013850080956884676)
XLA Ops:
  0.0 2.5 %collective-permute-start.2 = (s32[4,16]{1,0:T(4,128)}, s32[4,16]{1,0:T(4,128)S(1)}, u32[]{:S(2)}, u32[]{:S(2)}) collective-permute-start(s32[4,16]{1,0:T(4,128)} %bitcast.32), channel_id=1, source_target_pairs={{0,144},{1,145},{2,146},{3,147},{4,148},{5,149},{6,150},{7,151},{8... | collective-permute-start | bytes 776 | tf_op jit(solution)/shard_map/ppermute | solution.py:279
  2.5 3.6 %collective-permute-start.1 = (s32[4,16]{1,0:T(4,128)}, s32[4,16]{1,0:T(4,128)S(1)}, u32[]{:S(2)}, u32[]{:S(2)}) collective-permute-start(s32[4,16]{1,0:T(4,128)} %bitcast.33), channel_id=1, source_target_pairs={{0,145},{1,146},{2,147},{3,148},{4,149},{5,150},{6,151},{7,152},{8... | collective-permute-start | bytes 776 | tf_op jit(solution)/shard_map/ppermute | solution.py:279
  6.1 2.1 %fine_cart.1 = (f32[3,512,128]{2,1,0:T(8,128)S(1)}, bf16[3,512,128]{2,1,0:T(8,128)(2,1)S(1)}, f32[10,256,128]{2,1,0:T(8,128)S(1)}) custom-call(f32[1024,128]{1,0:T(8,128)} %bitcast.36, f32[1024,128]{1,0:T(8,128)} %bitcast.37, f32[10,256,128]{2,1,0:T(8,128)} %bitcast.35), custom_call_target="tpu_custom_call" | custom-call | flops 20000000000 | bytes 72000000 | tf_op jit(solution)/shard_map/fine_cart/pallas_call | solution.py:243
  8.2 0.1 member_sum.1
  8.3 0.1 collective-permute-start.5
  8.4 0.3 collective-permute-start
  8.7 0.0 collective-permute-done.2.r16_ref
  8.7 0.0 collective-permute-done.1.r17_ref
  8.7 0.0 copy-start
  8.7 0.7 %pick_rows.1 = (bf16[48,256]{1,0:T(8,128)(2,1)S(1)}, bf16[48,256]{1,0:T(8,128)(2,1)S(1)}) custom-call(s32[4,16]{1,0:T(4,128)S(1)} %collective-permute-done.1.r17_ref, s32[4,16]{1,0:T(4,128)S(1)} %collective-permute-done.2.r16_ref, f32[3,512,128]{2,1,0:T(8,128)S(1)} %get-tuple-element.18.cart_ref), custom_call_target="tpu_custom_call" | custom-call | flops 20000000000 | bytes 72000000 | tf_op jit(solution)/shard_map/pick_rows/pallas_call | solution.py:243
  9.4 2.4 %collective-permute-start.4 = (bf16[48,256]{1,0:T(8,128)(2,1)S(1)}, bf16[48,256]{1,0:T(8,128)(2,1)S(1)}, u32[]{:S(2)}, u32[]{:S(2)}) collective-permute-start(bf16[48,256]{1,0:T(8,128)(2,1)S(1)} %get-tuple-element.24), channel_id=1, source_target_pairs={{144,0},{145,1},{146,2},{147,3},{148,4},{149,5},{150,6},{151,7},{1... | collective-permute-start | bytes 73736 | tf_op jit(solution)/shard_map/ppermute | solution.py:311
  11.8 0.8 %collective-permute-start.3 = (bf16[48,256]{1,0:T(8,128)(2,1)S(1)}, bf16[48,256]{1,0:T(8,128)(2,1)S(1)}, u32[]{:S(2)}, u32[]{:S(2)}) collective-permute-start(bf16[48,256]{1,0:T(8,128)(2,1)S(1)} %get-tuple-element.23.after_ref), channel_id=1, source_target_pairs={{145,0},{146,1},{147,2},{148,3},{149,4},{150,5},{151,6},{152,7},{1... | collective-permute-start | bytes 73736 | tf_op jit(solution)/shard_map/ppermute | solution.py:311
  12.6 0.0 collective-permute-done.5.got_ref
  12.6 0.0 copy-start.2
  12.6 0.0 copy-start.3
  12.7 1.4 %collective-permute-start.6 = (f32[64,128]{1,0:T(8,128)S(1)}, f32[64,128]{1,0:T(8,128)S(1)}, u32[]{:S(2)}, u32[]{:S(2)}) collective-permute-start(f32[64,128]{1,0:T(8,128)S(1)} %get-tuple-element.28), channel_id=1, source_target_pairs={{0,32},{1,33},{2,34},{3,35},{4,36},{5,37},{6,38},{7,39},{8,40},{9,... | collective-permute-start | bytes 98312 | tf_op jit(solution)/shard_map/ppermute | solution.py:266
  14.0 0.0 collective-permute-done.below_ref
  14.0 0.0 copy-done
  14.0 0.0 copy-done.2
  14.0 0.0 copy-done.3
  14.1 0.0 copy-start.1
  14.1 1.2 %near_slots.1 = (f32[48,128]{1,0:T(8,128)S(1)}, f32[48,128]{1,0:T(8,128)S(1)}, f32[48,128]{1,0:T(8,128)S(1)}) custom-call(s32[4,16]{1,0:T(4,128)S(1)} %bitcast.34, s32[1,16]{1,0:T(1,128)S(1)} %copy-done.3, f32[3,512,128]{2,1,0:T(8,128)S(1)} %get-tuple-element.18.cart_ref, bf16[3,512,128]{2,1,0:T(8,128)(2,1)S(1)} %collective-permute-done.below_ref, ...), custom_call_target="tpu_custom_call" | custom-call | flops 20000000000 | bytes 72000000 | tf_op jit(solution)/shard_map/near_slots/pallas_call | solution.py:243
  15.3 0.0 collective-permute-done.4.g16_ref
  15.3 3.1 %collective-permute-done.3.g17_ref = bf16[48,256]{1,0:T(8,128)(2,1)S(1)} collective-permute-done((bf16[48,256]{1,0:T(8,128)(2,1)S(1)}, bf16[48,256]{1,0:T(8,128)(2,1)S(1)}, u32[]{:S(2)}, u32[]{:S(2)}) %collective-permute-start.3) | collective-permute-done | bytes 24608 | tf_op jit(solution)/shard_map/ppermute | solution.py:311
  18.4 0.0 collective-permute-done.6.got_ref
  18.4 0.0 copy-done.1
  18.4 0.3 far_slots.1
  18.6 12.4 %all_to_all.5.all_ref = f32[8,96,128]{2,1,0:T(8,128)S(1)} all-to-all(f32[8,96,128]{2,1,0:T(8,128)S(1)} %far_slots.1), channel_id=1, replica_groups=mesh['mem'=8,'tile'=32] {'mem'}, dimensions={0} | all-to-all | bytes 786432 | tf_op jit(solution)/shard_map/all_to_all | solution.py:332
  31.1 1.2 %recentre.1 = f32[10,256,128]{2,1,0:T(8,128)} custom-call(f32[10,256,128]{2,1,0:T(8,128)S(1)} %get-tuple-element.17.members_ref, f32[8,96,128]{2,1,0:T(8,128)S(1)} %all_to_all.5.all_ref), custom_call_target="tpu_custom_call" | custom-call | flops 1000000000 | bytes 3600000 | tf_op jit(solution)/shard_map/recentre/pallas_call | solution.py:243
  (1 shorter events, 0.0 us)
Async XLA Ops:
  0.0 8.7 %collective-permute-start.2 = (s32[4,16]{1,0:T(4,128)}, s32[4,16]{1,0:T(4,128)S(1)}, u32[]{:S(2)}, u32[]{:S(2)}) collective-permute-start(s32[4,16]{1,0:T(4,128)} %bitcast.32), channel_id=1, source_target_pairs={{0,144},{1,145},{2,146},{3,147},{4,148},{5,149},{6,150},{7,151},{8... | collective-permute-start | bytes 776 | tf_op jit(solution)/shard_map/ppermute | solution.py:279
  2.5 6.2 %collective-permute-start.1 = (s32[4,16]{1,0:T(4,128)}, s32[4,16]{1,0:T(4,128)S(1)}, u32[]{:S(2)}, u32[]{:S(2)}) collective-permute-start(s32[4,16]{1,0:T(4,128)} %bitcast.33), channel_id=1, source_target_pairs={{0,145},{1,146},{2,147},{3,148},{4,149},{5,150},{6,151},{7,152},{8... | collective-permute-start | bytes 776 | tf_op jit(solution)/shard_map/ppermute | solution.py:279
  8.3 4.4 %collective-permute-start.5 = (f32[128,128]{1,0:T(8,128)S(1)}, f32[128,128]{1,0:T(8,128)S(1)}, u32[]{:S(2)}, u32[]{:S(2)}) collective-permute-start(f32[128,128]{1,0:T(8,128)S(1)} %get-tuple-element.26), channel_id=1, source_target_pairs={{0,128},{1,129},{2,130},{3,131},{4,132},{5,133},{6,134},{7,135},{8... | collective-permute-start | bytes 196616 | tf_op jit(solution)/shard_map/ppermute | solution.py:266
  8.4 5.7 %collective-permute-start = (bf16[3,512,128]{2,1,0:T(8,128)(2,1)S(1)}, bf16[3,512,128]{2,1,0:T(8,128)(2,1)S(1)}, u32[]{:S(2)}, u32[]{:S(2)}) collective-permute-start(bf16[3,512,128]{2,1,0:T(8,128)(2,1)S(1)} %get-tuple-element.19), channel_id=1, source_target_pairs={{0,1},{1,2},{2,3},{3,4},{4,5},{5,6},{6,7},{7,8},{8,9},{9,10},{10,1... | collective-permute-start | bytes 1179656 | tf_op jit(solution)/shard_map/ppermute | solution.py:297
  8.7 5.4 %copy-start = (bf16[1,16,4,256,128]{4,3,2,1,0:T(8,128)(2,1)S(1)}, bf16[1,16,4,256,128]{4,3,2,1,0:T(8,128)(2,1)}, u32[]{:S(2)}) copy-start(bf16[1,16,4,256,128]{4,3,2,1,0:T(8,128)(2,1)} %param.11) | copy-start | bytes 12582916
  9.4 5.9 %collective-permute-start.4 = (bf16[48,256]{1,0:T(8,128)(2,1)S(1)}, bf16[48,256]{1,0:T(8,128)(2,1)S(1)}, u32[]{:S(2)}, u32[]{:S(2)}) collective-permute-start(bf16[48,256]{1,0:T(8,128)(2,1)S(1)} %get-tuple-element.24), channel_id=1, source_target_pairs={{144,0},{145,1},{146,2},{147,3},{148,4},{149,5},{150,6},{151,7},{1... | collective-permute-start | bytes 73736 | tf_op jit(solution)/shard_map/ppermute | solution.py:311
  11.8 6.6 %collective-permute-start.3 = (bf16[48,256]{1,0:T(8,128)(2,1)S(1)}, bf16[48,256]{1,0:T(8,128)(2,1)S(1)}, u32[]{:S(2)}, u32[]{:S(2)}) collective-permute-start(bf16[48,256]{1,0:T(8,128)(2,1)S(1)} %get-tuple-element.23.after_ref), channel_id=1, source_target_pairs={{145,0},{146,1},{147,2},{148,3},{149,4},{150,5},{151,6},{152,7},{1... | collective-permute-start | bytes 73736 | tf_op jit(solution)/shard_map/ppermute | solution.py:311
  12.6 1.4 %copy-start.2 = (s32[1,16,4]{1,2,0:T(4,128)S(1)}, s32[1,16,4]{1,2,0:T(4,128)}, u32[]{:S(2)}) copy-start(s32[1,16,4]{1,2,0:T(4,128)} %param.12) | copy-start | bytes 772
  12.6 1.4 %copy-start.3 = (s32[1,16]{1,0:T(1,128)S(1)}, s32[1,16]{1,0:T(1,128)}, u32[]{:S(2)}) copy-start(s32[1,16]{1,0:T(1,128)} %counts_ref.1) | copy-start | bytes 196
  12.7 5.7 %collective-permute-start.6 = (f32[64,128]{1,0:T(8,128)S(1)}, f32[64,128]{1,0:T(8,128)S(1)}, u32[]{:S(2)}, u32[]{:S(2)}) collective-permute-start(f32[64,128]{1,0:T(8,128)S(1)} %get-tuple-element.28), channel_id=1, source_target_pairs={{0,32},{1,33},{2,34},{3,35},{4,36},{5,37},{6,38},{7,39},{8,40},{9,... | collective-permute-start | bytes 98312 | tf_op jit(solution)/shard_map/ppermute | solution.py:266
  14.1 4.3 %copy-start.1 = (f32[2,16384]{1,0:T(2,128)S(1)}, f32[2,16384]{1,0:T(2,128)}, u32[]{:S(2)}) copy-start(f32[2,16384]{1,0:T(2,128)} %param.10) | copy-start | bytes 393220

commit v4 on v3

--- a/solution.py
+++ b/solution.py
@@ -56,40 +56,7 @@
         ref[...] = mine_ref[at, :] + got_ref[at, :]
 
 
-def cart_kernel(inc_hbm, ang_hbm, cart_ref, even_ref, inc, ang, sems):
-    parts = sems.shape[0]
-    step = inc.shape[0] // parts
-    loads = [
-        [pltpu.make_async_copy(src.at[split(n, parts, step)], dst.at[split(n, parts, step)], sems.at[n, k])
-         for k, (src, dst) in enumerate(((inc_hbm, inc), (ang_hbm, ang)))]
-        for n in range(parts)
-    ]
-    for pair in loads:
-        for load in pair:
-            load.start()
-    for n in range(parts):
-        for load in loads[n]:
-            load.wait()
-
-        def body(k, carry, n=n):
-            rows = 64
-            at = pl.ds(pl.multiple_of(n * step + k * rows, rows), rows)
-            s, c = sin_cos(ang[at, :].reshape(rows // 8, 8, 128))
-            u = inc[at, :].reshape(rows // 8, 8, 128)
-            su, cu = s * u, c * u
-            t = pltpu.roll(su, 7, 1)
-            cart_ref[0, at, :] = (-su - c * t).reshape(rows, 128)
-            cart_ref[1, at, :] = (cu - s * t).reshape(rows, 128)
-            cart_ref[2, at, :] = pltpu.roll(cu, 7, 1).reshape(rows, 128)
-            return carry
-
-        lax.fori_loop(0, step // 64, body, 0)
-        half = step // 2
-        for c in range(3):
-            even_ref[c, n * half : (n + 1) * half, :] = cart_ref[c, pl.ds(n * step, half, stride=2), :].astype(BF16)
-
-
-def first_kernel(inc_hbm, ang_hbm, members_hbm, cart_ref, even_ref, members_ref, inc, ang, odd, sems, member_sems):
+def first_kernel(inc_hbm, ang_hbm, members_hbm, even_ref, members_ref, inc, ang, odd, sems, member_sems):
     parts, count = sems.shape[0], members_hbm.shape[0]
     step = inc.shape[0] // parts
     loads = [
@@ -121,9 +88,7 @@
         lax.fori_loop(0, step // 64, body, 0)
         half = step // 2
         for c in range(3):
-            kept = odd[c, pl.ds(n * step, half, stride=2), :]
-            cart_ref[c, n * half : (n + 1) * half, :] = kept
-            even_ref[c, n * half : (n + 1) * half, :] = kept.astype(BF16)
+            even_ref[c, n * half : (n + 1) * half, :] = odd[c, pl.ds(n * step, half, stride=2), :].astype(BF16)
     for load in member_loads:
         load.wait()
 
@@ -135,74 +100,80 @@
     send_ref[...] = jnp.sum(members_ref[:, split(1 - half, 2, rows), :], axis=0)
 
 
-def pair_kernel(mine_ref, got_ref, after_ref, keep_ref, send_ref):
-    del after_ref
-    rows = keep_ref.shape[0]
-    half = lax.rem(lax.axis_index("mem"), 2)
-    for ref, part in ((keep_ref, half), (send_ref, 1 - half)):
-        at = split(part, 2, rows)
-        ref[...] = mine_ref[at, :] + got_ref[at, :]
-
-
-def pick_kernel(r17_ref, r16_ref, cart_ref, s17_ref, s16_ref, ids, tmp, sems):
-    fine = cart_ref.shape[1] // 2
-    asked = ((r17_ref, 3, s17_ref), (r16_ref, 3, s16_ref))
-    copies = [pltpu.make_async_copy(ref, ids.at[n], sems.at[n]) for n, (ref, _, _) in enumerate(asked)]
-    for copy in copies:
-        copy.start()
-    for copy in copies:
-        copy.wait()
-    for n, (ref, slot, out) in enumerate(asked):
-        for i in range(ref.shape[1]):
-            row = 2 * (ids[n, slot, i] & (fine - 1))
-            for c in range(3):
-                for h in range(2):
-                    tmp[n, 3 * i + c : 3 * i + c + 1, 128 * h : 128 * h + 128] = cart_ref[c, pl.ds(row + h, 1), :]
-        out[...] = tmp[n].astype(BF16)
-
-
-def near_kernel(ids_ref, counts_ref, cart_ref, below_ref, weights_ref, acc_ref, m17_ref, m16_ref, near, below):
-    blocks = weights_ref.shape[0]
-    fine = cart_ref.shape[1] // 2
+def column(row):
+    n = row.shape[1]
+    wide = jnp.concatenate([row.astype(F32), jnp.zeros((1, 128 - n), F32)], axis=1)
+    return jnp.transpose(jnp.broadcast_to(wide, (8, 128)))[0:n, 0:1]
+
+
+def pick_kernel(r17_ref, r16_ref, even_ref, s17_ref, s16_ref):
+    rows, blocks = even_ref.shape[1], r17_ref.shape[1]
+    fine = rows // 2
+    asked = jnp.concatenate([2 * (ref[3:4, :] & (fine - 1)) + h for ref in (r17_ref, r16_ref) for h in range(2)], axis=1)
+    at = lax.broadcasted_iota(jnp.int32, (4 * blocks, rows), 1).astype(F32)
+    chosen = jnp.where(at == column(asked), F32(1.0), F32(0.0)).astype(BF16)
+    table = jnp.concatenate([even_ref[c] for c in range(3)], axis=1)
+    got = jnp.dot(chosen, table, preferred_element_type=F32)
+    for n, ref in enumerate((s17_ref, s16_ref)):
+        for c in range(3):
+            ref[2 * blocks * c : 2 * blocks * (c + 1), :] = (
+                got[2 * blocks * n : 2 * blocks * (n + 1), 128 * c : 128 * (c + 1)].astype(ref.dtype)
+            )
+
+
+def near_kernel(ids_ref, counts_ref, even_ref, below_ref, weights_ref, acc_ref, from_ref, near, held):
+    blocks, rows = weights_ref.shape[0], even_ref.shape[1]
+    fine = rows // 2
+    bits = fine.bit_length() - 1
     tiles = lax.axis_size("tile")
     tile = lax.axis_index("tile")
     across = lax.rem(tile + tiles // 2, tiles)
-    first = pl.multiple_of(lax.axis_index("mem") * (blocks * 4), 8)
-    below[...] = below_ref[...].astype(F32)
-    for k in range(2):
-        for c in range(3):
-            for h in range(2):
-                near[2 * k + h, pl.ds(c, blocks, stride=3), :] = (
-                    cart_ref[c, pl.ds(first + 2 * k + h, blocks, stride=4), :]
-                )
-    for i in range(blocks):
-        count, two, three = counts_ref[0, i], ids_ref[2, i], ids_ref[3, i]
-        row, mine, straight = 2 * (two & (fine - 1)), two // fine == tile, three // fine == across
-        for c in range(3):
-            for h in range(2):
-                got = jnp.where(mine, cart_ref[c, pl.ds(row + h, 1), :], below[c, pl.ds(row + h, 1), :])
-                near[4 + h, 3 * i + c : 3 * i + c + 1, :] = jnp.where(count > 2, got, 0.0)
-        at = slice(3 * i, 3 * i + 3)
-        flag = lambda yes: jnp.full((3, 128), jnp.where(yes, F32(1.0), F32(0.0)))
-        m17_ref[at, :] = flag((count > 3) & ~straight)
-        m16_ref[at, :] = flag((count > 3) & straight)
+    first = split(lax.axis_index("mem"), 8, 4 * blocks)
+    count, two, three = counts_ref[...], ids_ref[2:3, :], ids_ref[3:4, :]
+    row = 2 * (two & (fine - 1)) + jnp.where((two >> bits) == tile, 0, rows)
+    asked = [jnp.where(count > 2, row + h, -1) for h in range(2)]
+    source = jnp.where(count > 3, jnp.where((three >> bits) == across, 1, 2), 0)
+    numbers = column(jnp.concatenate(asked + [source], axis=1))
+    from_ref[...] = jnp.broadcast_to(numbers[2 * blocks :], from_ref.shape)
+    at = lax.broadcasted_iota(jnp.int32, (2 * blocks, 2 * rows), 1).astype(F32)
+    chosen = jnp.where(at == numbers[: 2 * blocks], F32(1.0), F32(0.0)).astype(BF16)
+    got = sum(
+        jnp.dot(
+            chosen[:, rows * n : rows * (n + 1)],
+            jnp.concatenate([ref[c] for c in range(3)], axis=1),
+            preferred_element_type=F32,
+        )
+        for n, ref in enumerate((even_ref, below_ref))
+    )
+    for c in range(3):
+        held[c] = even_ref[c, first, :].astype(F32)
+        for h in range(2):
+            for k in range(2):
+                near[2 * k + h, pl.ds(c, blocks, stride=3), :] = held[c, pl.ds(2 * k + h, blocks, stride=4), :]
+            near[4 + h, pl.ds(c, blocks, stride=3), :] = got[blocks * h : blocks * (h + 1), 128 * c : 128 * (c + 1)]
     for i in range(blocks):
         at = slice(3 * i, 3 * i + 3)
         lhs = jnp.concatenate([near[n, at, :] for n in range(6)], axis=1).astype(BF16)
         acc_ref[at, :] = jnp.dot(lhs, weights_ref[i, 0:3].reshape(768, 128), preferred_element_type=F32)
 
 
-def far_kernel(acc_ref, m17_ref, m16_ref, g17_ref, g16_ref, ang_ref, keep_ref, got_ref, weights_ref,
+def far_kernel(acc_ref, from_ref, g17_ref, g16_ref, ang_ref, keep_ref, got_ref, weights_ref,
                out_ref, rows, cart, wind):
     blocks, piece = weights_ref.shape[0], wind.shape[0]
-    wide = lambda ref: jnp.concatenate([ref[...], ref[...]], axis=1) > 0.5
-    rows[...] = jnp.where(
-        wide(m16_ref), g16_ref[...].astype(F32), jnp.where(wide(m17_ref), g17_ref[...].astype(F32), 0.0)
-    )
+    from17 = from_ref[...] > 1.5
+    from16 = (from_ref[...] > 0.5) & ~from17
+    for c in range(3):
+        for h in range(2):
+            at = slice(blocks * (2 * c + h), blocks * (2 * c + h + 1))
+            rows[h, pl.ds(c, blocks, stride=3), :] = jnp.where(
+                from16, g16_ref[at, :].astype(F32), jnp.where(from17, g17_ref[at, :].astype(F32), 0.0)
+            )
     for i in range(blocks):
         at = slice(3 * i, 3 * i + 3)
         cart[at, :] = acc_ref[at, :] + jnp.dot(
-            rows[at, :].astype(BF16), weights_ref[i, 3], preferred_element_type=F32
+            jnp.concatenate([rows[0, at, :], rows[1, at, :]], axis=1).astype(BF16),
+            weights_ref[i, 3],
+            preferred_element_type=F32,
         )
     x, y, z = (cart[pl.ds(c, blocks, stride=3), :] for c in range(3))
     first = lax.axis_index("mem") * piece
@@ -284,10 +255,10 @@
     piece = total_rows // mems
     row = lambda n, dtype=F32: ((n, 128), dtype)
     whole = (3, fine_rows // 2, 128)
-    cart, even, members_rows = call(
+    even, members_rows = call(
         first_kernel,
         "fine_cart",
-        [(whole, F32), (whole, BF16), (members_rows.shape, F32)],
+        [(whole, BF16), (members_rows.shape, F32)],
         [HBM] * 3,
         [pltpu.VMEM(inc_rows.shape, F32)] * 2
         + [pltpu.VMEM((3, fine_rows, 128), F32), pltpu.SemaphoreType.DMA((4, 2)), pltpu.SemaphoreType.DMA((count,))],
@@ -299,35 +270,28 @@
     mine, other = call(sum_kernel, "member_sum", [row(4 * piece)] * 2, [VMEM], cost=20)(members_rows)
     got = send(other, flip, 0)
 
-    rows = ((3 * blocks, 256), BF16)
-    s17, s16 = call(
-        pick_kernel,
-        "pick_rows",
-        [rows] * 2,
-        [VMEM] * 3,
-        [pltpu.SMEM((2,) + ids.shape, jnp.int32), pltpu.VMEM((2, 3 * blocks, 256), F32), pltpu.SemaphoreType.DMA((2,))],
-        cost=20,
-    )(r17, r16, cart)
+    rows = (6 * blocks, 128)
+    s17, s16 = call(pick_kernel, "pick_rows", [(rows, BF16), (rows, BF16)], [VMEM] * 3, cost=2)(r17, r16, even)
     g17, g16 = (lax.ppermute(x, axes, [(d, a) for a, d in p]) for x, p in ((s17, p17), (s16, p16)))
 
-    keep, other = call(pair_kernel, "pair_sum", [row(2 * piece)] * 2, [VMEM, VMEM, ANY])(mine, got, s17)
+    keep, other = call(pair_kernel, "pair_sum", [row(2 * piece)] * 2, [VMEM, VMEM, ANY])(mine, got, s16)
     got = send(other, 1, 0)
 
     near = call(
         near_kernel,
         "near_slots",
-        [row(3 * blocks)] * 3,
-        [SMEM, SMEM, VMEM, VMEM, VMEM],
-        [pltpu.VMEM((6, 3 * blocks, 128), F32), pltpu.VMEM(whole, F32)],
+        [row(3 * blocks), row(blocks)],
+        [VMEM] * 5,
+        [pltpu.VMEM((6, 3 * blocks, 128), F32), pltpu.VMEM((3, 4 * blocks, 128), F32)],
         cost=20,
-    )(ids, counts, cart, below, weights)
+    )(ids, counts, even, below, weights)
 
     (payload,) = call(
         far_kernel,
         "far_slots",
         [((mems, 3 * piece, 128), F32)],
-        [VMEM] * 9,
-        [pltpu.VMEM((3 * blocks, 256), F32), pltpu.VMEM((3 * blocks, 128), F32), pltpu.VMEM((piece, 128), F32)],
+        [VMEM] * 8,
+        [pltpu.VMEM((2, 3 * blocks, 128), F32), pltpu.VMEM((3 * blocks, 128), F32), pltpu.VMEM((piece, 128), F32)],
     )(*near, g17, g16, flat(coarse_angles), keep, got, weights)
     payload = lax.all_to_all(payload, "mem", 0, 0, tiled=True)
     (out,) = call(

time: 32.4 us -> 31.8 us (0.981)
  the two profiles are of different devices: /device:TPU:97 before, /device:TPU:4 now
where the time goes in v4:
time: 31.8 us; the launch traced here: 31.7 us
  blocking collectives  14.7 us (46%)
  starting transfers between devices  10.5 us (33%)
  Pallas kernels  4.93 us (16%)
  waiting for transfers between devices  1.41 us (4%)
    all_to_all x1, blocking collectives, shards(): payload = lax.all_to_all(payload, 'mem', 0, 0, tiled=True)  14.7 us
    pallas_call x7, Pallas kernels, run(): pl.pallas_call(kernel, out_shape=shapes, in_specs=specs, out_specs=out_sp...  4.93 us
    ppermute x2, starting transfers between devices, send(): return lax.ppermute(x, ('mem', 'tile'), pairs)  4.16 us
    ppermute x2, starting transfers between devices, shards(): lax.ppermute(x, axes, [(d, a) for a, d in p])  2.77 us
    ppermute x1, starting transfers between devices, shards(): below = lax.ppermute(even, axes, shifted(1))  2.39 us
    ppermute x1, waiting for transfers between devices, shards(): below = lax.ppermute(even, axes, shifted(1))  1.39 us
    ppermute x2, starting transfers between devices, shards(): r17, r16 = (lax.ppermute(ids, axes, p) for p in (p17, p16))  1.19 us
  transfers between devices with their start and end apart: 7, of which 1 were waited for; matrix products, arithmetic and copies ran while one was open for 0% of the time, Pallas kernels for 11%

profile of v4, /device:TPU:4, one launch (start us, length us, event | category | flops | bytes accessed | tf_op | source)
XLA Modules:
  0.0 31.7 jit_solution(10448231041495192791)
XLA Ops:
  0.0 0.5 %collective-permute-start.2 = (s32[4,16]{1,0:T(4,128)}, s32[4,16]{1,0:T(4,128)S(1)}, u32[]{:S(2)}, u32[]{:S(2)}) collective-permute-start(s32[4,16]{1,0:T(4,128)} %bitcast.32), channel_id=1, source_target_pairs={{0,144},{1,145},{2,146},{3,147},{4,148},{5,149},{6,150},{7,151},{8... | collective-permute-start | bytes 776 | tf_op jit(solution)/shard_map/ppermute | solution.py:250
  0.5 0.7 %collective-permute-start.1 = (s32[4,16]{1,0:T(4,128)}, s32[4,16]{1,0:T(4,128)S(1)}, u32[]{:S(2)}, u32[]{:S(2)}) collective-permute-start(s32[4,16]{1,0:T(4,128)} %bitcast.33), channel_id=1, source_target_pairs={{0,145},{1,146},{2,147},{3,148},{4,149},{5,150},{6,151},{7,152},{8... | collective-permute-start | bytes 776 | tf_op jit(solution)/shard_map/ppermute | solution.py:250
  1.2 2.1 %fine_cart.1 = (bf16[3,512,128]{2,1,0:T(8,128)(2,1)S(1)}, f32[10,256,128]{2,1,0:T(8,128)S(1)}) custom-call(f32[1024,128]{1,0:T(8,128)} %bitcast.36, f32[1024,128]{1,0:T(8,128)} %bitcast.37, f32[10,256,128]{2,1,0:T(8,128)} %bitcast.35), custom_call_target="tpu_custom_call" | custom-call | flops 20000000000 | bytes 72000000 | tf_op jit(solution)/shard_map/fine_cart/pallas_call | solution.py:214
  3.3 2.4 %collective-permute-start = (bf16[3,512,128]{2,1,0:T(8,128)(2,1)S(1)}, bf16[3,512,128]{2,1,0:T(8,128)(2,1)S(1)}, u32[]{:S(2)}, u32[]{:S(2)}) collective-permute-start(bf16[3,512,128]{2,1,0:T(8,128)(2,1)S(1)} %get-tuple-element.16.even_ref), channel_id=1, source_target_pairs={{0,1},{1,2},{2,3},{3,4},{4,5},{5,6},{6,7},{7,8},{8,9},{9,10},{10,1... | collective-permute-start | bytes 1179656 | tf_op jit(solution)/shard_map/ppermute | solution.py:268
  5.7 0.1 member_sum.1
  5.7 2.5 %collective-permute-start.5 = (f32[128,128]{1,0:T(8,128)S(1)}, f32[128,128]{1,0:T(8,128)S(1)}, u32[]{:S(2)}, u32[]{:S(2)}) collective-permute-start(f32[128,128]{1,0:T(8,128)S(1)} %get-tuple-element.22), channel_id=1, source_target_pairs={{0,128},{1,129},{2,130},{3,131},{4,132},{5,133},{6,134},{7,135},{8... | collective-permute-start | bytes 196616 | tf_op jit(solution)/shard_map/ppermute | solution.py:237
  8.2 0.0 collective-permute-done.2.r16_ref
  8.2 0.0 collective-permute-done.1.r17_ref
  8.2 0.0 copy-start
  8.2 0.4 %pick_rows.1 = (bf16[96,128]{1,0:T(8,128)(2,1)S(1)}, bf16[96,128]{1,0:T(8,128)(2,1)S(1)}) custom-call(s32[4,16]{1,0:T(4,128)S(1)} %collective-permute-done.1.r17_ref, s32[4,16]{1,0:T(4,128)S(1)} %collective-permute-done.2.r16_ref, bf16[3,512,128]{2,1,0:T(8,128)(2,1)S(1)} %get-tuple-element.16.even_ref), custom_call_target="tpu_custom_call" | custom-call | flops 2000000000 | bytes 7200000 | tf_op jit(solution)/shard_map/pick_rows/pallas_call | solution.py:214
  8.6 1.2 %collective-permute-start.3 = (bf16[96,128]{1,0:T(8,128)(2,1)S(1)}, bf16[96,128]{1,0:T(8,128)(2,1)S(1)}, u32[]{:S(2)}, u32[]{:S(2)}) collective-permute-start(bf16[96,128]{1,0:T(8,128)(2,1)S(1)} %get-tuple-element.19), channel_id=1, source_target_pairs={{145,0},{146,1},{147,2},{148,3},{149,4},{150,5},{151,6},{152,7},{1... | collective-permute-start | bytes 73736 | tf_op jit(solution)/shard_map/ppermute | solution.py:275
  9.8 1.6 %collective-permute-start.4 = (bf16[96,128]{1,0:T(8,128)(2,1)S(1)}, bf16[96,128]{1,0:T(8,128)(2,1)S(1)}, u32[]{:S(2)}, u32[]{:S(2)}) collective-permute-start(bf16[96,128]{1,0:T(8,128)(2,1)S(1)} %get-tuple-element.20.after_ref), channel_id=1, source_target_pairs={{144,0},{145,1},{146,2},{147,3},{148,4},{149,5},{150,6},{151,7},{1... | collective-permute-start | bytes 73736 | tf_op jit(solution)/shard_map/ppermute | solution.py:275
  11.4 0.0 collective-permute-done.5.got_ref
  11.4 0.0 copy-start.2
  11.4 0.0 copy-start.3
  11.4 1.7 %collective-permute-start.6 = (f32[64,128]{1,0:T(8,128)S(1)}, f32[64,128]{1,0:T(8,128)S(1)}, u32[]{:S(2)}, u32[]{:S(2)}) collective-permute-start(f32[64,128]{1,0:T(8,128)S(1)} %get-tuple-element.24), channel_id=1, source_target_pairs={{0,32},{1,33},{2,34},{3,35},{4,36},{5,37},{6,38},{7,39},{8,40},{9,... | collective-permute-start | bytes 98312 | tf_op jit(solution)/shard_map/ppermute | solution.py:237
  13.1 1.4 %collective-permute-done.below_ref = bf16[3,512,128]{2,1,0:T(8,128)(2,1)S(1)} collective-permute-done((bf16[3,512,128]{2,1,0:T(8,128)(2,1)S(1)}, bf16[3,512,128]{2,1,0:T(8,128)(2,1)S(1)}, u32[]{:S(2)}, u32[]{:S(2)}) %collective-permute-start) | collective-permute-done | bytes 393248 | tf_op jit(solution)/shard_map/ppermute | solution.py:268
  14.5 0.0 copy-done
  14.5 0.0 copy-done.2
  14.5 0.0 copy-done.3
  14.5 0.0 copy-start.1
  14.5 1.0 %near_slots.1 = (f32[48,128]{1,0:T(8,128)S(1)}, f32[16,128]{1,0:T(8,128)S(1)}) custom-call(s32[4,16]{1,0:T(4,128)S(1)} %bitcast.34, s32[1,16]{1,0:T(1,128)S(1)} %copy-done.3, bf16[3,512,128]{2,1,0:T(8,128)(2,1)S(1)} %get-tuple-element.16.even_ref, bf16[3,512,128]{2,1,0:T(8,128)(2,1)S(1)} %collective-permute-done.below_ref, bf16[16,4,256,128]{3,2,1,0:T(8,128)(2,1)S(1)} %bitcast.29), custom_call_target="tpu_custom_call" | custom-call | flops 20000000000 | bytes 72000000 | tf_op jit(solution)/shard_map/near_slots/pallas_call | solution.py:214
  15.5 0.0 collective-permute-done.3.g17_ref
  15.5 0.0 collective-permute-done.4.g16_ref
  15.5 0.0 collective-permute-done.6.got_ref
  15.5 0.0 copy-done.1
  15.5 0.3 far_slots.1
  15.8 14.7 %all_to_all.5.all_ref = f32[8,96,128]{2,1,0:T(8,128)S(1)} all-to-all(f32[8,96,128]{2,1,0:T(8,128)S(1)} %far_slots.1), channel_id=1, replica_groups=mesh['mem'=8,'tile'=32] {'mem'}, dimensions={0} | all-to-all | bytes 786432 | tf_op jit(solution)/shard_map/all_to_all | solution.py:296
  30.5 1.2 %recentre.1 = f32[10,256,128]{2,1,0:T(8,128)} custom-call(f32[10,256,128]{2,1,0:T(8,128)S(1)} %get-tuple-element.15.members_ref, f32[8,96,128]{2,1,0:T(8,128)S(1)} %all_to_all.5.all_ref), custom_call_target="tpu_custom_call" | custom-call | flops 1000000000 | bytes 3600000 | tf_op jit(solution)/shard_map/recentre/pallas_call | solution.py:214
  (1 shorter events, 0.0 us)
Async XLA Ops:
  0.0 8.2 %collective-permute-start.2 = (s32[4,16]{1,0:T(4,128)}, s32[4,16]{1,0:T(4,128)S(1)}, u32[]{:S(2)}, u32[]{:S(2)}) collective-permute-start(s32[4,16]{1,0:T(4,128)} %bitcast.32), channel_id=1, source_target_pairs={{0,144},{1,145},{2,146},{3,147},{4,148},{5,149},{6,150},{7,151},{8... | collective-permute-start | bytes 776 | tf_op jit(solution)/shard_map/ppermute | solution.py:250
  0.5 7.7 %collective-permute-start.1 = (s32[4,16]{1,0:T(4,128)}, s32[4,16]{1,0:T(4,128)S(1)}, u32[]{:S(2)}, u32[]{:S(2)}) collective-permute-start(s32[4,16]{1,0:T(4,128)} %bitcast.33), channel_id=1, source_target_pairs={{0,145},{1,146},{2,147},{3,148},{4,149},{5,150},{6,151},{7,152},{8... | collective-permute-start | bytes 776 | tf_op jit(solution)/shard_map/ppermute | solution.py:250
  3.3 11.2 %collective-permute-start = (bf16[3,512,128]{2,1,0:T(8,128)(2,1)S(1)}, bf16[3,512,128]{2,1,0:T(8,128)(2,1)S(1)}, u32[]{:S(2)}, u32[]{:S(2)}) collective-permute-start(bf16[3,512,128]{2,1,0:T(8,128)(2,1)S(1)} %get-tuple-element.16.even_ref), channel_id=1, source_target_pairs={{0,1},{1,2},{2,3},{3,4},{4,5},{5,6},{6,7},{7,8},{8,9},{9,10},{10,1... | collective-permute-start | bytes 1179656 | tf_op jit(solution)/shard_map/ppermute | solution.py:268
  5.7 5.7 %collective-permute-start.5 = (f32[128,128]{1,0:T(8,128)S(1)}, f32[128,128]{1,0:T(8,128)S(1)}, u32[]{:S(2)}, u32[]{:S(2)}) collective-permute-start(f32[128,128]{1,0:T(8,128)S(1)} %get-tuple-element.22), channel_id=1, source_target_pairs={{0,128},{1,129},{2,130},{3,131},{4,132},{5,133},{6,134},{7,135},{8... | collective-permute-start | bytes 196616 | tf_op jit(solution)/shard_map/ppermute | solution.py:237
  8.2 6.2 %copy-start = (bf16[1,16,4,256,128]{4,3,2,1,0:T(8,128)(2,1)S(1)}, bf16[1,16,4,256,128]{4,3,2,1,0:T(8,128)(2,1)}, u32[]{:S(2)}) copy-start(bf16[1,16,4,256,128]{4,3,2,1,0:T(8,128)(2,1)} %param.11) | copy-start | bytes 12582916
  8.6 6.8 %collective-permute-start.3 = (bf16[96,128]{1,0:T(8,128)(2,1)S(1)}, bf16[96,128]{1,0:T(8,128)(2,1)S(1)}, u32[]{:S(2)}, u32[]{:S(2)}) collective-permute-start(bf16[96,128]{1,0:T(8,128)(2,1)S(1)} %get-tuple-element.19), channel_id=1, source_target_pairs={{145,0},{146,1},{147,2},{148,3},{149,4},{150,5},{151,6},{152,7},{1... | collective-permute-start | bytes 73736 | tf_op jit(solution)/shard_map/ppermute | solution.py:275
  9.8 5.6 %collective-permute-start.4 = (bf16[96,128]{1,0:T(8,128)(2,1)S(1)}, bf16[96,128]{1,0:T(8,128)(2,1)S(1)}, u32[]{:S(2)}, u32[]{:S(2)}) collective-permute-start(bf16[96,128]{1,0:T(8,128)(2,1)S(1)} %get-tuple-element.20.after_ref), channel_id=1, source_target_pairs={{144,0},{145,1},{146,2},{147,3},{148,4},{149,5},{150,6},{151,7},{1... | collective-permute-start | bytes 73736 | tf_op jit(solution)/shard_map/ppermute | solution.py:275
  11.4 3.1 %copy-start.2 = (s32[1,16,4]{1,2,0:T(4,128)S(1)}, s32[1,16,4]{1,2,0:T(4,128)}, u32[]{:S(2)}) copy-start(s32[1,16,4]{1,2,0:T(4,128)} %param.12) | copy-start | bytes 772
  11.4 3.1 %copy-start.3 = (s32[1,16]{1,0:T(1,128)S(1)}, s32[1,16]{1,0:T(1,128)}, u32[]{:S(2)}) copy-start(s32[1,16]{1,0:T(1,128)} %counts_ref.1) | copy-start | bytes 196
  11.4 4.1 %collective-permute-start.6 = (f32[64,128]{1,0:T(8,128)S(1)}, f32[64,128]{1,0:T(8,128)S(1)}, u32[]{:S(2)}, u32[]{:S(2)}) collective-permute-start(f32[64,128]{1,0:T(8,128)S(1)} %get-tuple-element.24), channel_id=1, source_target_pairs={{0,32},{1,33},{2,34},{3,35},{4,36},{5,37},{6,38},{7,39},{8,40},{9,... | collective-permute-start | bytes 98312 | tf_op jit(solution)/shard_map/ppermute | solution.py:237
  14.5 1.0 %copy-start.1 = (f32[2,16384]{1,0:T(2,128)S(1)}, f32[2,16384]{1,0:T(2,128)}, u32[]{:S(2)}) copy-start(f32[2,16384]{1,0:T(2,128)} %param.10) | copy-start | bytes 393220

commit v5 on v4

--- a/solution.py
+++ b/solution.py
@@ -57,7 +57,8 @@
 
 
 def first_kernel(inc_hbm, ang_hbm, members_hbm, even_ref, members_ref, inc, ang, odd, sems, member_sems):
-    parts, count = sems.shape[0], members_hbm.shape[0]
+    parts, groups = sems.shape[0], member_sems.shape[0]
+    each = members_hbm.shape[0] // groups
     step = inc.shape[0] // parts
     loads = [
         [pltpu.make_async_copy(src.at[split(n, parts, step)], dst.at[split(n, parts, step)], sems.at[n, k])
@@ -65,7 +66,8 @@
         for n in range(parts)
     ]
     member_loads = [
-        pltpu.make_async_copy(members_hbm.at[n], members_ref.at[n], member_sems.at[n]) for n in range(count)
+        pltpu.make_async_copy(members_hbm.at[pl.ds(each * n, each)], members_ref.at[pl.ds(each * n, each)], member_sems.at[n])
+        for n in range(groups)
     ]
     for load in sum(loads, []) + member_loads:
         load.start()
@@ -196,11 +198,16 @@
             for n in range(2):
                 at = slice((first + n) * piece, (first + n + 1) * piece)
                 delta[at, :] = all_ref[first + n, 0:piece, :] - mean[n * piece : (n + 1) * piece, :]
-    count = members_ref.shape[0]
-    copies = [pltpu.make_async_copy(buffer.at[i], out_ref.at[i], sems.at[i]) for i in range(count)]
-    for i in range(count):
-        buffer[i] = members_ref[i] + delta[...]
-        copies[i].start()
+    groups = sems.shape[0]
+    each = members_ref.shape[0] // groups
+    copies = [
+        pltpu.make_async_copy(buffer.at[pl.ds(each * n, each)], out_ref.at[pl.ds(each * n, each)], sems.at[n])
+        for n in range(groups)
+    ]
+    for n in range(groups):
+        for i in range(each * n, each * (n + 1)):
+            buffer[i] = members_ref[i] + delta[...]
+        copies[n].start()
     for copy in copies:
         copy.wait()
 
@@ -261,7 +268,7 @@
         [(whole, BF16), (members_rows.shape, F32)],
         [HBM] * 3,
         [pltpu.VMEM(inc_rows.shape, F32)] * 2
-        + [pltpu.VMEM((3, fine_rows, 128), F32), pltpu.SemaphoreType.DMA((4, 2)), pltpu.SemaphoreType.DMA((count,))],
+        + [pltpu.VMEM((3, fine_rows, 128), F32), pltpu.SemaphoreType.DMA((4, 2)), pltpu.SemaphoreType.DMA((1,))],
         cost=20,
     )(inc_rows, ang_rows, members_rows)
 
@@ -299,7 +306,7 @@
         "recentre",
         [(members_rows.shape, F32)],
         [VMEM, VMEM],
-        [pltpu.VMEM((total_rows, 128), F32), pltpu.VMEM(members_rows.shape, F32), pltpu.SemaphoreType.DMA((count,))],
+        [pltpu.VMEM((total_rows, 128), F32), pltpu.VMEM(members_rows.shape, F32), pltpu.SemaphoreType.DMA((1,))],
         pltpu.HBM,
     )(members_rows, payload)
     return unflat(out)

time: 31.8 us -> 31.7 us (level)
  transfers between devices with their start and end apart: 7 -> 7, of which waited for: 1 -> 1; matrix products, arithmetic and copies ran while one was open for 0% -> 0% of each run, Pallas kernels for 11% -> 10%
where the time goes in v5:
time: 31.7 us; the launch traced here: 31.5 us
  blocking collectives  14.8 us (47%)
  starting transfers between devices  10.5 us (33%)
  Pallas kernels  4.69 us (15%)
  waiting for transfers between devices  1.41 us (4%)
    all_to_all x1, blocking collectives, shards(): payload = lax.all_to_all(payload, 'mem', 0, 0, tiled=True)  14.8 us
    pallas_call x7, Pallas kernels, run(): pl.pallas_call(kernel, out_shape=shapes, in_specs=specs, out_specs=out_sp...  4.69 us
    ppermute x2, starting transfers between devices, send(): return lax.ppermute(x, ('mem', 'tile'), pairs)  4.16 us
    ppermute x2, starting transfers between devices, shards(): lax.ppermute(x, axes, [(d, a) for a, d in p])  2.77 us
    ppermute x1, starting transfers between devices, shards(): below = lax.ppermute(even, axes, shifted(1))  2.39 us
    ppermute x1, waiting for transfers between devices, shards(): below = lax.ppermute(even, axes, shifted(1))  1.39 us
    ppermute x2, starting transfers between devices, shards(): r17, r16 = (lax.ppermute(ids, axes, p) for p in (p17, p16))  1.19 us
  transfers between devices with their start and end apart: 7, of which 1 were waited for; matrix products, arithmetic and copies ran while one was open for 0% of the time, Pallas kernels for 10%

profile of v5, /device:TPU:4, one launch (start us, length us, event | category | flops | bytes accessed | tf_op | source)
XLA Modules:
  0.0 31.5 jit_solution(3271346780724195020)
XLA Ops:
  0.0 0.5 %collective-permute-start.2 = (s32[4,16]{1,0:T(4,128)}, s32[4,16]{1,0:T(4,128)S(1)}, u32[]{:S(2)}, u32[]{:S(2)}) collective-permute-start(s32[4,16]{1,0:T(4,128)} %bitcast.32), channel_id=1, source_target_pairs={{0,144},{1,145},{2,146},{3,147},{4,148},{5,149},{6,150},{7,151},{8... | collective-permute-start | bytes 776 | tf_op jit(solution)/shard_map/ppermute | solution.py:257
  0.5 0.7 %collective-permute-start.1 = (s32[4,16]{1,0:T(4,128)}, s32[4,16]{1,0:T(4,128)S(1)}, u32[]{:S(2)}, u32[]{:S(2)}) collective-permute-start(s32[4,16]{1,0:T(4,128)} %bitcast.33), channel_id=1, source_target_pairs={{0,145},{1,146},{2,147},{3,148},{4,149},{5,150},{6,151},{7,152},{8... | collective-permute-start | bytes 776 | tf_op jit(solution)/shard_map/ppermute | solution.py:257
  1.2 1.8 %fine_cart.1 = (bf16[3,512,128]{2,1,0:T(8,128)(2,1)S(1)}, f32[10,256,128]{2,1,0:T(8,128)S(1)}) custom-call(f32[1024,128]{1,0:T(8,128)} %bitcast.36, f32[1024,128]{1,0:T(8,128)} %bitcast.37, f32[10,256,128]{2,1,0:T(8,128)} %bitcast.35), custom_call_target="tpu_custom_call" | custom-call | flops 20000000000 | bytes 72000000 | tf_op jit(solution)/shard_map/fine_cart/pallas_call | solution.py:221
  3.0 2.4 %collective-permute-start = (bf16[3,512,128]{2,1,0:T(8,128)(2,1)S(1)}, bf16[3,512,128]{2,1,0:T(8,128)(2,1)S(1)}, u32[]{:S(2)}, u32[]{:S(2)}) collective-permute-start(bf16[3,512,128]{2,1,0:T(8,128)(2,1)S(1)} %get-tuple-element.16.even_ref), channel_id=1, source_target_pairs={{0,1},{1,2},{2,3},{3,4},{4,5},{5,6},{6,7},{7,8},{8,9},{9,10},{10,1... | collective-permute-start | bytes 1179656 | tf_op jit(solution)/shard_map/ppermute | solution.py:275
  5.4 0.1 member_sum.1
  5.5 2.5 %collective-permute-start.5 = (f32[128,128]{1,0:T(8,128)S(1)}, f32[128,128]{1,0:T(8,128)S(1)}, u32[]{:S(2)}, u32[]{:S(2)}) collective-permute-start(f32[128,128]{1,0:T(8,128)S(1)} %get-tuple-element.22), channel_id=1, source_target_pairs={{0,128},{1,129},{2,130},{3,131},{4,132},{5,133},{6,134},{7,135},{8... | collective-permute-start | bytes 196616 | tf_op jit(solution)/shard_map/ppermute | solution.py:244
  8.0 0.0 collective-permute-done.2.r16_ref
  8.0 0.0 collective-permute-done.1.r17_ref
  8.0 0.0 copy-start
  8.0 0.4 %pick_rows.1 = (bf16[96,128]{1,0:T(8,128)(2,1)S(1)}, bf16[96,128]{1,0:T(8,128)(2,1)S(1)}) custom-call(s32[4,16]{1,0:T(4,128)S(1)} %collective-permute-done.1.r17_ref, s32[4,16]{1,0:T(4,128)S(1)} %collective-permute-done.2.r16_ref, bf16[3,512,128]{2,1,0:T(8,128)(2,1)S(1)} %get-tuple-element.16.even_ref), custom_call_target="tpu_custom_call" | custom-call | flops 2000000000 | bytes 7200000 | tf_op jit(solution)/shard_map/pick_rows/pallas_call | solution.py:221
  8.4 1.5 %collective-permute-start.3 = (bf16[96,128]{1,0:T(8,128)(2,1)S(1)}, bf16[96,128]{1,0:T(8,128)(2,1)S(1)}, u32[]{:S(2)}, u32[]{:S(2)}) collective-permute-start(bf16[96,128]{1,0:T(8,128)(2,1)S(1)} %get-tuple-element.19), channel_id=1, source_target_pairs={{145,0},{146,1},{147,2},{148,3},{149,4},{150,5},{151,6},{152,7},{1... | collective-permute-start | bytes 73736 | tf_op jit(solution)/shard_map/ppermute | solution.py:282
  9.8 1.3 %collective-permute-start.4 = (bf16[96,128]{1,0:T(8,128)(2,1)S(1)}, bf16[96,128]{1,0:T(8,128)(2,1)S(1)}, u32[]{:S(2)}, u32[]{:S(2)}) collective-permute-start(bf16[96,128]{1,0:T(8,128)(2,1)S(1)} %get-tuple-element.20.after_ref), channel_id=1, source_target_pairs={{144,0},{145,1},{146,2},{147,3},{148,4},{149,5},{150,6},{151,7},{1... | collective-permute-start | bytes 73736 | tf_op jit(solution)/shard_map/ppermute | solution.py:282
  11.1 0.0 collective-permute-done.5.got_ref
  11.2 0.0 copy-start.2
  11.2 0.0 copy-start.3
  11.2 1.7 %collective-permute-start.6 = (f32[64,128]{1,0:T(8,128)S(1)}, f32[64,128]{1,0:T(8,128)S(1)}, u32[]{:S(2)}, u32[]{:S(2)}) collective-permute-start(f32[64,128]{1,0:T(8,128)S(1)} %get-tuple-element.24), channel_id=1, source_target_pairs={{0,32},{1,33},{2,34},{3,35},{4,36},{5,37},{6,38},{7,39},{8,40},{9,... | collective-permute-start | bytes 98312 | tf_op jit(solution)/shard_map/ppermute | solution.py:244
  12.8 1.4 %collective-permute-done.below_ref = bf16[3,512,128]{2,1,0:T(8,128)(2,1)S(1)} collective-permute-done((bf16[3,512,128]{2,1,0:T(8,128)(2,1)S(1)}, bf16[3,512,128]{2,1,0:T(8,128)(2,1)S(1)}, u32[]{:S(2)}, u32[]{:S(2)}) %collective-permute-start) | collective-permute-done | bytes 393248 | tf_op jit(solution)/shard_map/ppermute | solution.py:275
  14.2 0.0 copy-done
  14.2 0.0 copy-done.2
  14.2 0.0 copy-done.3
  14.2 0.0 copy-start.1
  14.2 1.0 %near_slots.1 = (f32[48,128]{1,0:T(8,128)S(1)}, f32[16,128]{1,0:T(8,128)S(1)}) custom-call(s32[4,16]{1,0:T(4,128)S(1)} %bitcast.34, s32[1,16]{1,0:T(1,128)S(1)} %copy-done.3, bf16[3,512,128]{2,1,0:T(8,128)(2,1)S(1)} %get-tuple-element.16.even_ref, bf16[3,512,128]{2,1,0:T(8,128)(2,1)S(1)} %collective-permute-done.below_ref, bf16[16,4,256,128]{3,2,1,0:T(8,128)(2,1)S(1)} %bitcast.29), custom_call_target="tpu_custom_call" | custom-call | flops 20000000000 | bytes 72000000 | tf_op jit(solution)/shard_map/near_slots/pallas_call | solution.py:221
  15.2 0.0 collective-permute-done.3.g17_ref
  15.2 0.0 collective-permute-done.4.g16_ref
  15.2 0.0 collective-permute-done.6.got_ref
  15.2 0.0 copy-done.1
  15.3 0.3 far_slots.1
  15.5 14.8 %all_to_all.5.all_ref = f32[8,96,128]{2,1,0:T(8,128)S(1)} all-to-all(f32[8,96,128]{2,1,0:T(8,128)S(1)} %far_slots.1), channel_id=1, replica_groups=mesh['mem'=8,'tile'=32] {'mem'}, dimensions={0} | all-to-all | bytes 786432 | tf_op jit(solution)/shard_map/all_to_all | solution.py:303
  30.3 1.2 %recentre.1 = f32[10,256,128]{2,1,0:T(8,128)} custom-call(f32[10,256,128]{2,1,0:T(8,128)S(1)} %get-tuple-element.15.members_ref, f32[8,96,128]{2,1,0:T(8,128)S(1)} %all_to_all.5.all_ref), custom_call_target="tpu_custom_call" | custom-call | flops 1000000000 | bytes 3600000 | tf_op jit(solution)/shard_map/recentre/pallas_call | solution.py:221
  (1 shorter events, 0.0 us)
Async XLA Ops:
  0.0 8.0 %collective-permute-start.2 = (s32[4,16]{1,0:T(4,128)}, s32[4,16]{1,0:T(4,128)S(1)}, u32[]{:S(2)}, u32[]{:S(2)}) collective-permute-start(s32[4,16]{1,0:T(4,128)} %bitcast.32), channel_id=1, source_target_pairs={{0,144},{1,145},{2,146},{3,147},{4,148},{5,149},{6,150},{7,151},{8... | collective-permute-start | bytes 776 | tf_op jit(solution)/shard_map/ppermute | solution.py:257
  0.5 7.4 %collective-permute-start.1 = (s32[4,16]{1,0:T(4,128)}, s32[4,16]{1,0:T(4,128)S(1)}, u32[]{:S(2)}, u32[]{:S(2)}) collective-permute-start(s32[4,16]{1,0:T(4,128)} %bitcast.33), channel_id=1, source_target_pairs={{0,145},{1,146},{2,147},{3,148},{4,149},{5,150},{6,151},{7,152},{8... | collective-permute-start | bytes 776 | tf_op jit(solution)/shard_map/ppermute | solution.py:257
  3.0 11.2 %collective-permute-start = (bf16[3,512,128]{2,1,0:T(8,128)(2,1)S(1)}, bf16[3,512,128]{2,1,0:T(8,128)(2,1)S(1)}, u32[]{:S(2)}, u32[]{:S(2)}) collective-permute-start(bf16[3,512,128]{2,1,0:T(8,128)(2,1)S(1)} %get-tuple-element.16.even_ref), channel_id=1, source_target_pairs={{0,1},{1,2},{2,3},{3,4},{4,5},{5,6},{6,7},{7,8},{8,9},{9,10},{10,1... | collective-permute-start | bytes 1179656 | tf_op jit(solution)/shard_map/ppermute | solution.py:275
  5.5 5.7 %collective-permute-start.5 = (f32[128,128]{1,0:T(8,128)S(1)}, f32[128,128]{1,0:T(8,128)S(1)}, u32[]{:S(2)}, u32[]{:S(2)}) collective-permute-start(f32[128,128]{1,0:T(8,128)S(1)} %get-tuple-element.22), channel_id=1, source_target_pairs={{0,128},{1,129},{2,130},{3,131},{4,132},{5,133},{6,134},{7,135},{8... | collective-permute-start | bytes 196616 | tf_op jit(solution)/shard_map/ppermute | solution.py:244
  8.0 6.2 %copy-start = (bf16[1,16,4,256,128]{4,3,2,1,0:T(8,128)(2,1)S(1)}, bf16[1,16,4,256,128]{4,3,2,1,0:T(8,128)(2,1)}, u32[]{:S(2)}) copy-start(bf16[1,16,4,256,128]{4,3,2,1,0:T(8,128)(2,1)} %param.11) | copy-start | bytes 12582916
  8.4 6.8 %collective-permute-start.3 = (bf16[96,128]{1,0:T(8,128)(2,1)S(1)}, bf16[96,128]{1,0:T(8,128)(2,1)S(1)}, u32[]{:S(2)}, u32[]{:S(2)}) collective-permute-start(bf16[96,128]{1,0:T(8,128)(2,1)S(1)} %get-tuple-element.19), channel_id=1, source_target_pairs={{145,0},{146,1},{147,2},{148,3},{149,4},{150,5},{151,6},{152,7},{1... | collective-permute-start | bytes 73736 | tf_op jit(solution)/shard_map/ppermute | solution.py:282
  9.8 5.4 %collective-permute-start.4 = (bf16[96,128]{1,0:T(8,128)(2,1)S(1)}, bf16[96,128]{1,0:T(8,128)(2,1)S(1)}, u32[]{:S(2)}, u32[]{:S(2)}) collective-permute-start(bf16[96,128]{1,0:T(8,128)(2,1)S(1)} %get-tuple-element.20.after_ref), channel_id=1, source_target_pairs={{144,0},{145,1},{146,2},{147,3},{148,4},{149,5},{150,6},{151,7},{1... | collective-permute-start | bytes 73736 | tf_op jit(solution)/shard_map/ppermute | solution.py:282
  11.2 3.1 %copy-start.2 = (s32[1,16,4]{1,2,0:T(4,128)S(1)}, s32[1,16,4]{1,2,0:T(4,128)}, u32[]{:S(2)}) copy-start(s32[1,16,4]{1,2,0:T(4,128)} %param.12) | copy-start | bytes 772
  11.2 3.1 %copy-start.3 = (s32[1,16]{1,0:T(1,128)S(1)}, s32[1,16]{1,0:T(1,128)}, u32[]{:S(2)}) copy-start(s32[1,16]{1,0:T(1,128)} %counts_ref.1) | copy-start | bytes 196
  11.2 4.1 %collective-permute-start.6 = (f32[64,128]{1,0:T(8,128)S(1)}, f32[64,128]{1,0:T(8,128)S(1)}, u32[]{:S(2)}, u32[]{:S(2)}) collective-permute-start(f32[64,128]{1,0:T(8,128)S(1)} %get-tuple-element.24), channel_id=1, source_target_pairs={{0,32},{1,33},{2,34},{3,35},{4,36},{5,37},{6,38},{7,39},{8,40},{9,... | collective-permute-start | bytes 98312 | tf_op jit(solution)/shard_map/ppermute | solution.py:244
  14.2 1.0 %copy-start.1 = (f32[2,16384]{1,0:T(2,128)S(1)}, f32[2,16384]{1,0:T(2,128)}, u32[]{:S(2)}) copy-start(f32[2,16384]{1,0:T(2,128)} %param.10) | copy-start | bytes 393220

commit v6 on v5

--- a/solution.py
+++ b/solution.py
@@ -56,7 +56,8 @@
         ref[...] = mine_ref[at, :] + got_ref[at, :]
 
 
-def first_kernel(inc_hbm, ang_hbm, members_hbm, even_ref, members_ref, inc, ang, odd, sems, member_sems):
+def first_kernel(inc_hbm, ang_hbm, members_hbm, even_ref, members_ref, keep_ref, send_ref,
+                 inc, ang, odd, sems, member_sems):
     parts, groups = sems.shape[0], member_sems.shape[0]
     each = members_hbm.shape[0] // groups
     step = inc.shape[0] // parts
@@ -93,13 +94,10 @@
             even_ref[c, n * half : (n + 1) * half, :] = odd[c, pl.ds(n * step, half, stride=2), :].astype(BF16)
     for load in member_loads:
         load.wait()
-
-
-def sum_kernel(members_ref, keep_ref, send_ref):
-    rows = keep_ref.shape[0]
-    half = lax.axis_index("mem") // 4
-    keep_ref[...] = jnp.sum(members_ref[:, split(half, 2, rows), :], axis=0)
-    send_ref[...] = jnp.sum(members_ref[:, split(1 - half, 2, rows), :], axis=0)
+    held = keep_ref.shape[0]
+    group = lax.axis_index("mem") // 4
+    send_ref[...] = jnp.sum(members_ref[:, split(1 - group, 2, held), :], axis=0)
+    keep_ref[...] = jnp.sum(members_ref[:, split(group, 2, held), :], axis=0)
 
 
 def column(row):
@@ -262,10 +260,10 @@
     piece = total_rows // mems
     row = lambda n, dtype=F32: ((n, 128), dtype)
     whole = (3, fine_rows // 2, 128)
-    even, members_rows = call(
+    even, members_rows, mine, other = call(
         first_kernel,
         "fine_cart",
-        [(whole, BF16), (members_rows.shape, F32)],
+        [(whole, BF16), (members_rows.shape, F32)] + [row(4 * piece)] * 2,
         [HBM] * 3,
         [pltpu.VMEM(inc_rows.shape, F32)] * 2
         + [pltpu.VMEM((3, fine_rows, 128), F32), pltpu.SemaphoreType.DMA((4, 2)), pltpu.SemaphoreType.DMA((1,))],
@@ -274,11 +272,10 @@
 
     below = lax.ppermute(even, axes, shifted(1))
 
-    mine, other = call(sum_kernel, "member_sum", [row(4 * piece)] * 2, [VMEM], cost=20)(members_rows)
     got = send(other, flip, 0)
 
     rows = (6 * blocks, 128)
-    s17, s16 = call(pick_kernel, "pick_rows", [(rows, BF16), (rows, BF16)], [VMEM] * 3, cost=2)(r17, r16, even)
+    s17, s16 = call(pick_kernel, "pick_rows", [(rows, BF16), (rows, BF16)], [VMEM] * 3, cost=20)(r17, r16, even)
     g17, g16 = (lax.ppermute(x, axes, [(d, a) for a, d in p]) for x, p in ((s17, p17), (s16, p16)))
 
     keep, other = call(pair_kernel, "pair_sum", [row(2 * piece)] * 2, [VMEM, VMEM, ANY])(mine, got, s16)

time: 31.7 us -> 31.7 us (level)
  waiting for transfers between devices: 1.41 us -> 3.1 us
  blocking collectives: 14.8 us -> 13.2 us
    ppermute x1, waiting for transfers between devices: 1.39 us -> 3.08 us  [shards(): below = lax.ppermute(even, axes, shifted(1))]
    all_to_all x1, blocking collectives: 14.8 us -> 13.2 us  [shards(): payload = lax.all_to_all(payload, 'mem', 0, 0, tiled=True)]
    ppermute x1, starting transfers between devices: 2.39 us -> 2.03 us  [shards(): below = lax.ppermute(even, axes, shifted(1))]
    pallas_call x7 -> x6, Pallas kernels: 4.69 us -> 4.69 us  [run(): pl.pallas_call(kernel, out_shape=shapes, in_specs=specs, out_specs=out_sp...]
where the time goes in v6:
time: 31.7 us; the launch traced here: 31.5 us
  blocking collectives  13.2 us (42%)
  starting transfers between devices  10.4 us (33%)
  Pallas kernels  4.69 us (15%)
  waiting for transfers between devices  3.1 us (10%)
    all_to_all x1, blocking collectives, shards(): payload = lax.all_to_all(payload, 'mem', 0, 0, tiled=True)  13.2 us
    pallas_call x6, Pallas kernels, run(): pl.pallas_call(kernel, out_shape=shapes, in_specs=specs, out_specs=out_sp...  4.69 us
    ppermute x2, starting transfers between devices, send(): return lax.ppermute(x, ('mem', 'tile'), pairs)  4.16 us
    ppermute x1, waiting for transfers between devices, shards(): below = lax.ppermute(even, axes, shifted(1))  3.08 us
    ppermute x2, starting transfers between devices, shards(): lax.ppermute(x, axes, [(d, a) for a, d in p])  3.03 us
    ppermute x1, starting transfers between devices, shards(): below = lax.ppermute(even, axes, shifted(1))  2.03 us
    ppermute x2, starting transfers between devices, shards(): r17, r16 = (lax.ppermute(ids, axes, p) for p in (p17, p16))  1.19 us
  transfers between devices with their start and end apart: 7, of which 1 were waited for; matrix products, arithmetic and copies ran while one was open for 0% of the time, Pallas kernels for 10%

profile of v6, /device:TPU:4, one launch (start us, length us, event | category | flops | bytes accessed | tf_op | source)
XLA Modules:
  0.0 31.5 jit_solution(13010480925220019442)
XLA Ops:
  0.0 0.5 %collective-permute-start.2 = (s32[4,16]{1,0:T(4,128)}, s32[4,16]{1,0:T(4,128)S(1)}, u32[]{:S(2)}, u32[]{:S(2)}) collective-permute-start(s32[4,16]{1,0:T(4,128)} %bitcast.32), channel_id=1, source_target_pairs={{0,144},{1,145},{2,146},{3,147},{4,148},{5,149},{6,150},{7,151},{8... | collective-permute-start | bytes 776 | tf_op jit(solution)/shard_map/ppermute | solution.py:255
  0.5 0.7 %collective-permute-start.1 = (s32[4,16]{1,0:T(4,128)}, s32[4,16]{1,0:T(4,128)S(1)}, u32[]{:S(2)}, u32[]{:S(2)}) collective-permute-start(s32[4,16]{1,0:T(4,128)} %bitcast.33), channel_id=1, source_target_pairs={{0,145},{1,146},{2,147},{3,148},{4,149},{5,150},{6,151},{7,152},{8... | collective-permute-start | bytes 776 | tf_op jit(solution)/shard_map/ppermute | solution.py:255
  1.2 1.9 %fine_cart.1 = (bf16[3,512,128]{2,1,0:T(8,128)(2,1)S(1)}, f32[10,256,128]{2,1,0:T(8,128)S(1)}, f32[128,128]{1,0:T(8,128)S(1)}, f32[128,128]{1,0:T(8,128)S(1)}) custom-call(f32[1024,128]{1,0:T(8,128)} %bitcast.36, f32[1024,128]{1,0:T(8,128)} %bitcast.37, f32[10,256,128]{2,1,0:T(8,128)} %bitcast.35), custom_call_target="tpu_custom_call" | custom-call | flops 20000000000 | bytes 72000000 | tf_op jit(solution)/shard_map/fine_cart/pallas_call | solution.py:219
  3.1 2.5 %collective-permute-start.5 = (f32[128,128]{1,0:T(8,128)S(1)}, f32[128,128]{1,0:T(8,128)S(1)}, u32[]{:S(2)}, u32[]{:S(2)}) collective-permute-start(f32[128,128]{1,0:T(8,128)S(1)} %get-tuple-element.22), channel_id=1, source_target_pairs={{0,128},{1,129},{2,130},{3,131},{4,132},{5,133},{6,134},{7,135},{8... | collective-permute-start | bytes 196616 | tf_op jit(solution)/shard_map/ppermute | solution.py:242
  5.6 2.0 %collective-permute-start = (bf16[3,512,128]{2,1,0:T(8,128)(2,1)S(1)}, bf16[3,512,128]{2,1,0:T(8,128)(2,1)S(1)}, u32[]{:S(2)}, u32[]{:S(2)}) collective-permute-start(bf16[3,512,128]{2,1,0:T(8,128)(2,1)S(1)} %get-tuple-element.16.even_ref), channel_id=1, source_target_pairs={{0,1},{1,2},{2,3},{3,4},{4,5},{5,6},{6,7},{7,8},{8,9},{9,10},{10,1... | collective-permute-start | bytes 1179656 | tf_op jit(solution)/shard_map/ppermute | solution.py:273
  7.6 0.0 collective-permute-done.2.r16_ref
  7.6 0.0 collective-permute-done.1.r17_ref
  7.6 0.0 copy-start
  7.6 0.4 %pick_rows.1 = (bf16[96,128]{1,0:T(8,128)(2,1)S(1)}, bf16[96,128]{1,0:T(8,128)(2,1)S(1)}) custom-call(s32[4,16]{1,0:T(4,128)S(1)} %collective-permute-done.1.r17_ref, s32[4,16]{1,0:T(4,128)S(1)} %collective-permute-done.2.r16_ref, bf16[3,512,128]{2,1,0:T(8,128)(2,1)S(1)} %get-tuple-element.16.even_ref), custom_call_target="tpu_custom_call" | custom-call | flops 20000000000 | bytes 72000000 | tf_op jit(solution)/shard_map/pick_rows/pallas_call | solution.py:219
  8.0 1.8 %collective-permute-start.3 = (bf16[96,128]{1,0:T(8,128)(2,1)S(1)}, bf16[96,128]{1,0:T(8,128)(2,1)S(1)}, u32[]{:S(2)}, u32[]{:S(2)}) collective-permute-start(bf16[96,128]{1,0:T(8,128)(2,1)S(1)} %get-tuple-element.19), channel_id=1, source_target_pairs={{145,0},{146,1},{147,2},{148,3},{149,4},{150,5},{151,6},{152,7},{1... | collective-permute-start | bytes 73736 | tf_op jit(solution)/shard_map/ppermute | solution.py:279
  9.8 1.2 %collective-permute-start.4 = (bf16[96,128]{1,0:T(8,128)(2,1)S(1)}, bf16[96,128]{1,0:T(8,128)(2,1)S(1)}, u32[]{:S(2)}, u32[]{:S(2)}) collective-permute-start(bf16[96,128]{1,0:T(8,128)(2,1)S(1)} %get-tuple-element.20.after_ref), channel_id=1, source_target_pairs={{144,0},{145,1},{146,2},{147,3},{148,4},{149,5},{150,6},{151,7},{1... | collective-permute-start | bytes 73736 | tf_op jit(solution)/shard_map/ppermute | solution.py:279
  11.0 0.0 collective-permute-done.5.got_ref
  11.0 0.0 copy-start.2
  11.1 0.0 copy-start.3
  11.1 1.7 %collective-permute-start.6 = (f32[64,128]{1,0:T(8,128)S(1)}, f32[64,128]{1,0:T(8,128)S(1)}, u32[]{:S(2)}, u32[]{:S(2)}) collective-permute-start(f32[64,128]{1,0:T(8,128)S(1)} %get-tuple-element.24), channel_id=1, source_target_pairs={{0,32},{1,33},{2,34},{3,35},{4,36},{5,37},{6,38},{7,39},{8,40},{9,... | collective-permute-start | bytes 98312 | tf_op jit(solution)/shard_map/ppermute | solution.py:242
  12.7 3.1 %collective-permute-done.below_ref = bf16[3,512,128]{2,1,0:T(8,128)(2,1)S(1)} collective-permute-done((bf16[3,512,128]{2,1,0:T(8,128)(2,1)S(1)}, bf16[3,512,128]{2,1,0:T(8,128)(2,1)S(1)}, u32[]{:S(2)}, u32[]{:S(2)}) %collective-permute-start) | collective-permute-done | bytes 393248 | tf_op jit(solution)/shard_map/ppermute | solution.py:273
  15.8 0.0 copy-done
  15.8 0.0 copy-done.2
  15.8 0.0 copy-done.3
  15.8 0.0 copy-start.1
  15.8 1.0 %near_slots.1 = (f32[48,128]{1,0:T(8,128)S(1)}, f32[16,128]{1,0:T(8,128)S(1)}) custom-call(s32[4,16]{1,0:T(4,128)S(1)} %bitcast.34, s32[1,16]{1,0:T(1,128)S(1)} %copy-done.3, bf16[3,512,128]{2,1,0:T(8,128)(2,1)S(1)} %get-tuple-element.16.even_ref, bf16[3,512,128]{2,1,0:T(8,128)(2,1)S(1)} %collective-permute-done.below_ref, bf16[16,4,256,128]{3,2,1,0:T(8,128)(2,1)S(1)} %bitcast.29), custom_call_target="tpu_custom_call" | custom-call | flops 20000000000 | bytes 72000000 | tf_op jit(solution)/shard_map/near_slots/pallas_call | solution.py:219
  16.8 0.0 collective-permute-done.3.g17_ref
  16.8 0.0 collective-permute-done.4.g16_ref
  16.8 0.0 collective-permute-done.6.got_ref
  16.8 0.0 copy-done.1
  16.8 0.3 far_slots.1
  17.1 13.2 %all_to_all.5.all_ref = f32[8,96,128]{2,1,0:T(8,128)S(1)} all-to-all(f32[8,96,128]{2,1,0:T(8,128)S(1)} %far_slots.1), channel_id=1, replica_groups=mesh['mem'=8,'tile'=32] {'mem'}, dimensions={0} | all-to-all | bytes 786432 | tf_op jit(solution)/shard_map/all_to_all | solution.py:300
  30.3 1.2 %recentre.1 = f32[10,256,128]{2,1,0:T(8,128)} custom-call(f32[10,256,128]{2,1,0:T(8,128)S(1)} %get-tuple-element.15.members_ref, f32[8,96,128]{2,1,0:T(8,128)S(1)} %all_to_all.5.all_ref), custom_call_target="tpu_custom_call" | custom-call | flops 1000000000 | bytes 3600000 | tf_op jit(solution)/shard_map/recentre/pallas_call | solution.py:219
  (1 shorter events, 0.0 us)
Async XLA Ops:
  0.0 7.6 %collective-permute-start.2 = (s32[4,16]{1,0:T(4,128)}, s32[4,16]{1,0:T(4,128)S(1)}, u32[]{:S(2)}, u32[]{:S(2)}) collective-permute-start(s32[4,16]{1,0:T(4,128)} %bitcast.32), channel_id=1, source_target_pairs={{0,144},{1,145},{2,146},{3,147},{4,148},{5,149},{6,150},{7,151},{8... | collective-permute-start | bytes 776 | tf_op jit(solution)/shard_map/ppermute | solution.py:255
  0.5 7.1 %collective-permute-start.1 = (s32[4,16]{1,0:T(4,128)}, s32[4,16]{1,0:T(4,128)S(1)}, u32[]{:S(2)}, u32[]{:S(2)}) collective-permute-start(s32[4,16]{1,0:T(4,128)} %bitcast.33), channel_id=1, source_target_pairs={{0,145},{1,146},{2,147},{3,148},{4,149},{5,150},{6,151},{7,152},{8... | collective-permute-start | bytes 776 | tf_op jit(solution)/shard_map/ppermute | solution.py:255
  3.1 8.0 %collective-permute-start.5 = (f32[128,128]{1,0:T(8,128)S(1)}, f32[128,128]{1,0:T(8,128)S(1)}, u32[]{:S(2)}, u32[]{:S(2)}) collective-permute-start(f32[128,128]{1,0:T(8,128)S(1)} %get-tuple-element.22), channel_id=1, source_target_pairs={{0,128},{1,129},{2,130},{3,131},{4,132},{5,133},{6,134},{7,135},{8... | collective-permute-start | bytes 196616 | tf_op jit(solution)/shard_map/ppermute | solution.py:242
  5.6 10.2 %collective-permute-start = (bf16[3,512,128]{2,1,0:T(8,128)(2,1)S(1)}, bf16[3,512,128]{2,1,0:T(8,128)(2,1)S(1)}, u32[]{:S(2)}, u32[]{:S(2)}) collective-permute-start(bf16[3,512,128]{2,1,0:T(8,128)(2,1)S(1)} %get-tuple-element.16.even_ref), channel_id=1, source_target_pairs={{0,1},{1,2},{2,3},{3,4},{4,5},{5,6},{6,7},{7,8},{8,9},{9,10},{10,1... | collective-permute-start | bytes 1179656 | tf_op jit(solution)/shard_map/ppermute | solution.py:273
  7.6 8.2 %copy-start = (bf16[1,16,4,256,128]{4,3,2,1,0:T(8,128)(2,1)S(1)}, bf16[1,16,4,256,128]{4,3,2,1,0:T(8,128)(2,1)}, u32[]{:S(2)}) copy-start(bf16[1,16,4,256,128]{4,3,2,1,0:T(8,128)(2,1)} %param.11) | copy-start | bytes 12582916
  8.0 8.8 %collective-permute-start.3 = (bf16[96,128]{1,0:T(8,128)(2,1)S(1)}, bf16[96,128]{1,0:T(8,128)(2,1)S(1)}, u32[]{:S(2)}, u32[]{:S(2)}) collective-permute-start(bf16[96,128]{1,0:T(8,128)(2,1)S(1)} %get-tuple-element.19), channel_id=1, source_target_pairs={{145,0},{146,1},{147,2},{148,3},{149,4},{150,5},{151,6},{152,7},{1... | collective-permute-start | bytes 73736 | tf_op jit(solution)/shard_map/ppermute | solution.py:279
  9.8 7.0 %collective-permute-start.4 = (bf16[96,128]{1,0:T(8,128)(2,1)S(1)}, bf16[96,128]{1,0:T(8,128)(2,1)S(1)}, u32[]{:S(2)}, u32[]{:S(2)}) collective-permute-start(bf16[96,128]{1,0:T(8,128)(2,1)S(1)} %get-tuple-element.20.after_ref), channel_id=1, source_target_pairs={{144,0},{145,1},{146,2},{147,3},{148,4},{149,5},{150,6},{151,7},{1... | collective-permute-start | bytes 73736 | tf_op jit(solution)/shard_map/ppermute | solution.py:279
  11.0 4.8 %copy-start.2 = (s32[1,16,4]{1,2,0:T(4,128)S(1)}, s32[1,16,4]{1,2,0:T(4,128)}, u32[]{:S(2)}) copy-start(s32[1,16,4]{1,2,0:T(4,128)} %param.12) | copy-start | bytes 772
  11.1 4.8 %copy-start.3 = (s32[1,16]{1,0:T(1,128)S(1)}, s32[1,16]{1,0:T(1,128)}, u32[]{:S(2)}) copy-start(s32[1,16]{1,0:T(1,128)} %counts_ref.1) | copy-start | bytes 196
  11.1 5.8 %collective-permute-start.6 = (f32[64,128]{1,0:T(8,128)S(1)}, f32[64,128]{1,0:T(8,128)S(1)}, u32[]{:S(2)}, u32[]{:S(2)}) collective-permute-start(f32[64,128]{1,0:T(8,128)S(1)} %get-tuple-element.24), channel_id=1, source_target_pairs={{0,32},{1,33},{2,34},{3,35},{4,36},{5,37},{6,38},{7,39},{8,40},{9,... | collective-permute-start | bytes 98312 | tf_op jit(solution)/shard_map/ppermute | solution.py:242
  15.8 1.0 %copy-start.1 = (f32[2,16384]{1,0:T(2,128)S(1)}, f32[2,16384]{1,0:T(2,128)}, u32[]{:S(2)}) copy-start(f32[2,16384]{1,0:T(2,128)} %param.10) | copy-start | bytes 393220
